TPU v7x, 32 devices: a whole 2x2x4 slice. The times are simulated.
32 devices in a mesh: segment: 4 (over y, x), dp: 8 (over z, core).
Axes of the slice: x: 2, y: 2, z: 4, core: 2. Of those that a mesh axis runs over, the one named last changes fastest.
Arguments:
- tokens: bfloat16 [16, 512, 768], P('dp'), may hold values from -6 to 6
- group_ids: int32 [16, 512], P('dp'), may hold values from 0 to 2, as said below
- type_ids: int32 [16, 512], P('dp'), may hold values from 0 to 1, as said below
- norm_gain: bfloat16 [4, 768], P('segment'), may hold values from 0.5 to 1.5
- norm_bias: bfloat16 [4, 768], P('segment'), may hold values from -1.75 to 1.75
- qkv_weight: bfloat16 [2, 768, 2304], replicated, may hold values from -0.21875 to 0.21875
- qv_bias: bfloat16 [2, 2, 768], replicated, may hold values from -1.75 to 1.75
- out_weight: bfloat16 [2, 768, 768], replicated, may hold values from -1.75 to 1.75
- out_bias: bfloat16 [2, 768], replicated, may hold values from -1.75 to 1.75
- up_weight: bfloat16 [3, 768, 3072], replicated, may hold values from -0.21875 to 0.21875
- up_bias: bfloat16 [3, 3072], replicated, may hold values from -1.75 to 1.75
- down_weight: bfloat16 [3, 3072, 768], replicated, may hold values from -0.109375 to 0.109375
- down_bias: bfloat16 [3, 768], replicated, may hold values from -1.75 to 1.75
- out_cotangent: bfloat16 [16, 512, 768], P('dp'), may hold values from -8 to 8
Outputs:
- layer_output: bfloat16 [16, 512, 768], P('dp', 'segment')
- input_grad: float32 [16, 512, 768], P('dp', 'segment')
- norm_gain_grad: float32 [4, 768], P('segment', 'dp')
- norm_bias_grad: float32 [4, 768], P('segment', 'dp')
- qkv_weight_grad: float32 [2, 768, 2304], P(None, 'dp')
- qv_bias_grad: float32 [2, 2, 768], P(None, None, 'dp')
- out_weight_grad: float32 [2, 768, 768], P(None, 'dp')
- out_bias_grad: float32 [2, 768], P(None, 'dp')
- up_weight_grad: float32 [3, 768, 3072], P(None, 'dp')
- up_bias_grad: float32 [3, 3072], P(None, 'dp')
- down_weight_grad: float32 [3, 3072, 768], P(None, 'dp')
- down_bias_grad: float32 [3, 768], P(None, 'dp')
Inputs may be any that keep to these rules, and one draw needn't show every extreme that they name: `group_ids`: in each row of 512 tokens the group numbers never fall and all three occur: group 0 is text, group 1 is one item of 197 image tokens followed by 1 to 3 captions of 64 tokens, group 2 is text. `type_ids`: in each row, type 0 marks exactly the first 197 tokens of group 1, one unbroken run; every other token is 1.
All inputs are finite; a program needn't handle non-finite values.
Results may differ from a plain program's by a relative error of at most 0.014.
Values may be sent and summed in bfloat16 or wider, within the bound.
A program may use at most 512 MiB of HBM per device.

v0:
```python
from functools import partial
import math

import jax
import jax.numpy as jnp
from jax import lax
from jax.sharding import PartitionSpec as P

D = 768
H = 12
HD = 64
FF = 3072
PATCHES = 197


def shortened(value):

    def short(part):
        return part.astype(jnp.bfloat16) if part.dtype == jnp.float32 else part

    return jax.tree.map(short, value)


def shifted_2(value, axis, steps):
    count = lax.axis_size(axis)
    leading, last = (max(0, -steps), min(count, count - steps))
    return lax.ppermute(value, axis, [(source, source + steps) for source in range(leading, last)])


def spread_2(value, axis, root):
    mine = lax.axis_index(axis) == root
    return lax.psum(jnp.where(mine, value, jnp.zeros_like(value)), axis)


def normalize(values, scale_row, shift_row):
    center = values - jnp.mean(values, axis=-1, keepdims=True)
    spread = jnp.mean(center * center, axis=-1, keepdims=True)
    return center * lax.rsqrt(spread + 1e-05) * scale_row + shift_row


def smooth_gelu(values):
    return (
        0.5
        * values
        * (1.0 + jnp.tanh(0.7978845608028654 * (values + 0.044715 * values * values * values)))
    )


def text_rows(image_start, row_count):
    text_spots = jnp.arange(row_count - PATCHES, dtype=jnp.int32)
    return text_spots + jnp.where(text_spots >= image_start, PATCHES, 0).astype(jnp.int32)


def split_routes(values, image_start, text_index):
    return (
        lax.dynamic_slice_in_dim(values, image_start, PATCHES, 0),
        jnp.take(values, text_index, axis=0),
    )


def place_rows(image_part, text_part, image_start, text_index):
    merged = jnp.zeros(
        (image_part.shape[0] + text_part.shape[0], image_part.shape[1]), image_part.dtype
    )
    merged = merged.at[text_index].set(text_part)
    return lax.dynamic_update_slice_in_dim(merged, image_part, image_start, 0)


def attention_forward(hidden, same_group, scale_row, shift_row, weight_set):
    qkv_proj, qv_shift, out_proj, out_shift = weight_set
    row_count = hidden.shape[0]
    attn_in = normalize(hidden, scale_row, shift_row).astype(jnp.bfloat16)
    zero_bias = jnp.zeros((D,), jnp.float32)
    bias_row = jnp.concatenate(
        [qv_shift[0].astype(jnp.float32), zero_bias, qv_shift[1].astype(jnp.float32)]
    )
    projected = (jnp.dot(attn_in, qkv_proj, preferred_element_type=jnp.float32) + bias_row).astype(
        jnp.bfloat16
    )
    queries = projected[:, :D].reshape(row_count, H, HD)
    keys_part = projected[:, D : 2 * D].reshape(row_count, H, HD)
    values_part = projected[:, 2 * D :].reshape(row_count, H, HD)
    scores = jnp.einsum(
        "qhd,khd->hqk", queries, keys_part, preferred_element_type=jnp.float32
    ) * HD ** (-0.5)
    scores = jnp.where(same_group[None], scores, -1e30)
    shifted = scores - jnp.max(scores, axis=-1, keepdims=True)
    exponent = jnp.exp(shifted)
    attention = exponent / jnp.sum(exponent, axis=-1, keepdims=True)
    attention_low = attention.astype(jnp.bfloat16)
    context = jnp.einsum(
        "hqk,khd->qhd", attention_low, values_part, preferred_element_type=jnp.float32
    )
    context = context.reshape(row_count, D).astype(jnp.bfloat16)
    result_block = hidden + (
        jnp.dot(context, out_proj, preferred_element_type=jnp.float32)
        + out_shift.astype(jnp.float32)
    )
    return (
        result_block,
        (attn_in, queries, keys_part, values_part, attention, attention_low, context),
    )


def attention_backward(grad_low, hidden, same_group, scale_row, shift_row, weight_set):
    qkv_proj, qv_shift, out_proj, out_shift = weight_set
    _, kept_values = attention_forward(hidden, same_group, scale_row, shift_row, weight_set)
    attn_in, queries, keys_part, values_part, attention, attention_low, context = kept_values
    row_count = hidden.shape[0]
    grad_out = grad_low.astype(jnp.float32)
    out_proj_grad = jnp.einsum("rd,re->de", context, grad_low, preferred_element_type=jnp.float32)
    out_shift_grad = jnp.sum(grad_out, axis=0)
    context_grad = jnp.einsum("re,de->rd", grad_low, out_proj, preferred_element_type=jnp.float32)
    context_grad = context_grad.astype(jnp.bfloat16).reshape(row_count, H, HD)
    values_grad = jnp.einsum(
        "hqk,qhd->khd", attention_low, context_grad, preferred_element_type=jnp.float32
    )
    attention_grad = jnp.einsum(
        "qhd,khd->hqk", context_grad, values_part, preferred_element_type=jnp.float32
    )
    scores_grad = attention * (
        attention_grad - jnp.sum(attention_grad * attention, axis=-1, keepdims=True)
    )
    scores_grad = scores_grad.astype(jnp.bfloat16)
    queries_grad = jnp.einsum(
        "hqk,khd->qhd", scores_grad, keys_part, preferred_element_type=jnp.float32
    ) * HD ** (-0.5)
    keys_grad = jnp.einsum(
        "hqk,qhd->khd", scores_grad, queries, preferred_element_type=jnp.float32
    ) * HD ** (-0.5)
    projected_grad = jnp.concatenate(
        [
            queries_grad.reshape(row_count, D),
            keys_grad.reshape(row_count, D),
            values_grad.reshape(row_count, D),
        ],
        axis=1,
    ).astype(jnp.bfloat16)
    qv_shift_grad = jnp.stack(
        [
            jnp.sum(projected_grad[:, :D].astype(jnp.float32), axis=0),
            jnp.sum(projected_grad[:, 2 * D :].astype(jnp.float32), axis=0),
        ]
    )
    qkv_proj_grad = jnp.einsum(
        "rd,re->de", attn_in, projected_grad, preferred_element_type=jnp.float32
    )
    attn_in_grad = jnp.einsum(
        "re,de->rd", projected_grad, qkv_proj, preferred_element_type=jnp.float32
    )
    hidden_part, scale_grad, shift_grad = jax.vjp(normalize, hidden, scale_row, shift_row)[1](
        attn_in_grad
    )
    return (
        grad_out + hidden_part,
        [scale_grad, shift_grad, qkv_proj_grad, qv_shift_grad, out_proj_grad, out_shift_grad],
    )


def expert_inputs(ffn_in, image_start, routed):
    row_count = ffn_in.shape[0]
    text_index = text_rows(image_start, row_count)
    if not routed:
        return ((ffn_in,), text_index)
    return (split_routes(ffn_in, image_start, text_index), text_index)


def expert_forward(hidden, image_start, scale_row, shift_row, weight_set):
    up_proj, up_shift, down_proj, down_shift, routed = weight_set
    ffn_in = normalize(hidden, scale_row, shift_row).astype(jnp.bfloat16)
    inputs, text_index = expert_inputs(ffn_in, image_start, routed)
    pre_acts = tuple(
        (
            jnp.dot(inputs[expert], up_proj[expert], preferred_element_type=jnp.float32)
            + up_shift[expert].astype(jnp.float32)
            for expert in range(len(inputs))
        )
    )
    activated = tuple((smooth_gelu(pre_act).astype(jnp.bfloat16) for pre_act in pre_acts))
    expert_outs = tuple(
        (
            jnp.dot(activated[expert], down_proj[expert], preferred_element_type=jnp.float32)
            + down_shift[expert].astype(jnp.float32)
            for expert in range(len(inputs))
        )
    )
    if not routed:
        joined = expert_outs[0]
    else:
        joined = place_rows(expert_outs[0], expert_outs[1], image_start, text_index)
    return (hidden + joined, (inputs, pre_acts, activated, text_index))


def expert_backward(grad_low, hidden, image_start, scale_row, shift_row, weight_set):
    up_proj, up_shift, down_proj, down_shift, routed = weight_set
    _, kept_values = expert_forward(hidden, image_start, scale_row, shift_row, weight_set)
    inputs, pre_acts, activated, text_index = kept_values
    grad_out = grad_low.astype(jnp.float32)
    if not routed:
        grad_parts = (grad_low,)
    else:
        grad_parts = split_routes(grad_low, image_start, text_index)
    up_grads, up_shift_grads, down_grads, down_shift_grads, input_grads = ([], [], [], [], [])
    for expert in range(len(inputs)):
        expert_grad = grad_parts[expert]
        down_grads.append(
            jnp.einsum(
                "rf,rd->fd", activated[expert], expert_grad, preferred_element_type=jnp.float32
            )
        )
        down_shift_grads.append(jnp.sum(expert_grad.astype(jnp.float32), axis=0))
        act_grad = jnp.einsum(
            "rd,fd->rf", expert_grad, down_proj[expert], preferred_element_type=jnp.float32
        )
        pre_grad = jax.vjp(smooth_gelu, pre_acts[expert])[1](act_grad)[0].astype(jnp.bfloat16)
        up_grads.append(
            jnp.einsum("rd,rf->df", inputs[expert], pre_grad, preferred_element_type=jnp.float32)
        )
        up_shift_grads.append(jnp.sum(pre_grad.astype(jnp.float32), axis=0))
        input_grads.append(
            jnp.einsum("rf,df->rd", pre_grad, up_proj[expert], preferred_element_type=jnp.float32)
        )
    if not routed:
        ffn_in_grad = input_grads[0]
    else:
        ffn_in_grad = place_rows(input_grads[0], input_grads[1], image_start, text_index)
    hidden_part, scale_grad, shift_grad = jax.vjp(normalize, hidden, scale_row, shift_row)[1](
        ffn_in_grad
    )
    return (
        grad_out + hidden_part,
        [
            scale_grad,
            shift_grad,
            jnp.stack(up_grads),
            jnp.stack(up_shift_grads),
            jnp.stack(down_grads),
            jnp.stack(down_shift_grads),
        ],
    )


def attention_layout():
    return [((D,), 0), ((D,), 0), ((D, 3 * D), 0), ((2, D), 1), ((D, D), 0), ((D,), 0)]


def expert_layout(experts_here):
    return [
        ((D,), 0),
        ((D,), 0),
        ((experts_here, D, FF), 1),
        ((experts_here, FF), 1),
        ((experts_here, FF, D), 1),
        ((experts_here, D), 1),
    ]


def section_layouts():
    return [attention_layout(), expert_layout(2), attention_layout(), expert_layout(1)]


def layout_entries(layout):
    return sum((math.prod(full_shape) for full_shape, split_dim in layout))


def padded_width(entries):
    return -(-entries // 128) * 128


def split_rows(grad_term, split_dim, group_count):
    full_shape = grad_term.shape
    pieces_all = grad_term.reshape(
        full_shape[:split_dim]
        + (group_count, full_shape[split_dim] // group_count)
        + full_shape[split_dim + 1 :]
    )
    return jnp.moveaxis(pieces_all, split_dim, 0).reshape(group_count, -1)


def fit_width(flat_terms, width):
    return jnp.pad(flat_terms, ((0, 0), (0, width - flat_terms.shape[1])))


def pack_terms(grad_terms, layout, group_count, pack_width):
    flat_terms = jnp.concatenate(
        [
            split_rows(grad_term, split_dim, group_count)
            for grad_term, (full_shape, split_dim) in zip(grad_terms, layout)
        ],
        axis=1,
    )
    return fit_width(flat_terms, pack_width)


def unpack_row(flat_row, layout, group_count):
    results = []
    offset = 0
    for full_shape, split_dim in layout:
        shard_shape = (
            full_shape[:split_dim]
            + (full_shape[split_dim] // group_count,)
            + full_shape[split_dim + 1 :]
        )
        entries = math.prod(shard_shape)
        results.append(flat_row[offset : offset + entries].reshape(shard_shape))
        offset = offset + entries
    return results


def per_device(
    tokens,
    group_ids,
    type_ids,
    norm_gain,
    norm_bias,
    qkv_weight,
    qv_bias,
    out_weight,
    out_bias,
    up_weight,
    up_bias,
    down_weight,
    down_bias,
    out_cotangent,
):
    segment_count = lax.axis_size("segment")
    segment_place = lax.axis_index("segment")
    group_count = lax.axis_size("dp")
    micro_count = tokens.shape[0]
    row_count = tokens.shape[1]
    tick_count = micro_count + segment_count - 1
    scale_row = norm_gain[0].astype(jnp.float32)
    shift_row = norm_bias[0].astype(jnp.float32)
    layouts = section_layouts()
    pack_width = padded_width(max((layout_entries(layout) for layout in layouts)) // group_count)
    same_all = group_ids[:, :, None] == group_ids[:, None, :]
    row_spots = jnp.arange(row_count, dtype=jnp.int32)[None, :]
    image_starts = jnp.min(jnp.where(type_ids == 0, row_spots, row_count), axis=1)
    attention_sets = tuple(
        (
            (
                qkv_weight[layer_index],
                qv_bias[layer_index],
                out_weight[layer_index],
                out_bias[layer_index],
            )
            for layer_index in range(2)
        )
    )
    expert_sets = (
        (up_weight[0:2], up_bias[0:2], down_weight[0:2], down_bias[0:2], True),
        (up_weight[2:3], up_bias[2:3], down_weight[2:3], down_bias[2:3], False),
    )

    def forward_branch(section, block_in, position):
        if section % 2 == 0:
            result_block = attention_forward(
                block_in, same_all[position], scale_row, shift_row, attention_sets[section // 2]
            )[0]
        else:
            result_block = expert_forward(
                block_in, image_starts[position], scale_row, shift_row, expert_sets[section // 2]
            )[0]
        return result_block.astype(jnp.bfloat16)

    def forward_tick(tick_index, loop_state):
        incoming, kept_inputs, finals = loop_state
        micro_index = tick_index - segment_place
        active = (micro_index >= 0) & (micro_index < micro_count)
        position = jnp.clip(micro_index, 0, micro_count - 1)
        given_block = jnp.where(segment_place == 0, tokens[position], incoming)

        def forward_compute(block_in):
            return lax.switch(
                segment_place,
                [partial(forward_branch, section) for section in range(segment_count)],
                block_in.astype(jnp.float32),
                position,
            )

        def forward_resting(block_in):
            return jnp.zeros_like(block_in)

        result_block = lax.cond(active, forward_compute, forward_resting, given_block)
        kept_inputs = kept_inputs.at[position].set(
            jnp.where(active, given_block, kept_inputs[position])
        )
        finals = finals.at[position].set(jnp.where(active, result_block, finals[position]))
        incoming = jax.tree.map(
            lambda part, own: part.astype(own.dtype),
            shifted_2(shortened(result_block), "segment", 1),
            result_block,
        )
        return (incoming, kept_inputs, finals)

    zero_block = jnp.zeros(tokens.shape[1:], jnp.bfloat16)
    stash_zero = jnp.zeros(tokens.shape, jnp.bfloat16)
    _, kept_inputs, finals = lax.fori_loop(
        0, tick_count, forward_tick, (zero_block, stash_zero, stash_zero)
    )

    def backward_branch(section, grad_low, position):
        hidden = kept_inputs[position].astype(jnp.float32)
        if section % 2 == 0:
            hidden_grad, grad_terms = attention_backward(
                grad_low,
                hidden,
                same_all[position],
                scale_row,
                shift_row,
                attention_sets[section // 2],
            )
        else:
            hidden_grad, grad_terms = expert_backward(
                grad_low,
                hidden,
                image_starts[position],
                scale_row,
                shift_row,
                expert_sets[section // 2],
            )
        return (hidden_grad, pack_terms(grad_terms, layouts[section], group_count, pack_width))

    def backward_tick(tick_index, loop_state):
        incoming, input_grads, totals = loop_state
        micro_index = tick_index - (segment_count - 1 - segment_place)
        active = (micro_index >= 0) & (micro_index < micro_count)
        position = jnp.clip(micro_index, 0, micro_count - 1)
        given_block = jnp.where(
            segment_place == segment_count - 1, out_cotangent[position], incoming
        )

        def backward_compute(block_in):
            return lax.switch(
                segment_place,
                [partial(backward_branch, section) for section in range(segment_count)],
                block_in,
                position,
            )

        def backward_resting(block_in):
            return (
                jnp.zeros(block_in.shape, jnp.float32),
                jnp.zeros((group_count, pack_width), jnp.float32),
            )

        hidden_grad, flat_terms = lax.cond(active, backward_compute, backward_resting, given_block)
        input_grads = input_grads.at[position].set(
            jnp.where(active, hidden_grad, input_grads[position])
        )
        totals = totals + flat_terms
        incoming = shifted_2(hidden_grad.astype(jnp.bfloat16), "segment", -1)
        return (incoming, input_grads, totals)

    grads_zero = jnp.zeros(tokens.shape, jnp.float32)
    totals_start = jnp.zeros((group_count, pack_width), jnp.float32)
    _, input_grads, totals = lax.fori_loop(
        0, tick_count, backward_tick, (zero_block, grads_zero, totals_start)
    )
    width_d = D // group_count
    shares = lax.psum_scatter(totals, "dp", scatter_dimension=0, tiled=True)
    gathered = lax.all_gather(shares.astype(jnp.bfloat16), "segment", axis=0, tiled=True).astype(
        shares.dtype
    )
    norm_gain_grad = shares[0, :width_d].reshape(1, width_d)
    norm_bias_grad = shares[0, width_d : 2 * width_d].reshape(1, width_d)
    first_attention = unpack_row(gathered[0], layouts[0], group_count)
    both_experts = unpack_row(gathered[1], layouts[1], group_count)
    second_attention = unpack_row(gathered[2], layouts[2], group_count)
    uniting_expert = unpack_row(gathered[3], layouts[3], group_count)
    qkv_weight_grad = jnp.stack([first_attention[2], second_attention[2]])
    qv_bias_grad = jnp.stack([first_attention[3], second_attention[3]])
    out_weight_grad = jnp.stack([first_attention[4], second_attention[4]])
    out_bias_grad = jnp.stack([first_attention[5], second_attention[5]])
    up_weight_grad = jnp.concatenate([both_experts[2], uniting_expert[2]], axis=0)
    up_bias_grad = jnp.concatenate([both_experts[3], uniting_expert[3]], axis=0)
    down_weight_grad = jnp.concatenate([both_experts[4], uniting_expert[4]], axis=0)
    down_bias_grad = jnp.concatenate([both_experts[5], uniting_expert[5]], axis=0)
    own_rows = row_count // segment_count
    final_all = spread_2(finals, "segment", segment_count - 1)
    input_all = spread_2(input_grads.astype(jnp.bfloat16), "segment", 0).astype(input_grads.dtype)
    layer_output = lax.dynamic_slice_in_dim(final_all, segment_place * own_rows, own_rows, 1)
    input_grad = lax.dynamic_slice_in_dim(input_all, segment_place * own_rows, own_rows, 1)
    return (
        layer_output,
        input_grad,
        norm_gain_grad,
        norm_bias_grad,
        qkv_weight_grad,
        qv_bias_grad,
        out_weight_grad,
        out_bias_grad,
        up_weight_grad,
        up_bias_grad,
        down_weight_grad,
        down_bias_grad,
    )


def solution(mesh):
    return jax.shard_map(
        per_device,
        mesh=mesh,
        in_specs=(
            P("dp", None, None),
            P("dp", None),
            P("dp", None),
            P("segment", None),
            P("segment", None),
            P(),
            P(),
            P(),
            P(),
            P(),
            P(),
            P(),
            P(),
            P("dp", None, None),
        ),
        out_specs=(
            P("dp", "segment", None),
            P("dp", "segment", None),
            P("segment", "dp"),
            P("segment", "dp"),
            P(None, "dp", None),
            P(None, None, "dp"),
            P(None, "dp", None),
            P(None, "dp"),
            P(None, "dp", None),
            P(None, "dp"),
            P(None, "dp", None),
            P(None, "dp"),
        ),
        check_vma=False,
    )
```

profile of v0, /device:TPU:0, one launch (start us, length us, event | category | flops | bytes accessed | tf_op | source)
XLA Modules:
  0.0 2642.8 jit_solution(6711734944224306102)
XLA Ops:
  42.8 294.1 %while.41 = (s32[]{:T(128)}, bf16[512,768]{1,0:T(8,128)(2,1)S(1)}, bf16[2,512,768]{2,1,0:T(8,128)(2,1)S(1)}, bf16[2,512,768]{2,1,0:T(8,128)(2,1)}, s32[]{:T(128)...) while((s32[]{:T(128)}, bf16[512,768]{1,0:T(8,128)(2,1)S(1)}, ...), condition=%wide.region_22.24_spmd.clone, body=%wide.region_1.23_spmd.clone.sunk | while | flops 4855427072 | bytes 77062736 | solution.py:398
  68.9 37.6 %conditional.16 = (bf16[512,768]{1,0:T(8,128)(2,1)}) conditional(s32[]{:T(128)} %convert_element_type.603, () %tuple.214, (s32[]{:T(128)}, bf16[512,768]{1,0:T(8,128)(2,1)}, f32[768]{0:T(1024)S(1)}, f32[768]{0:T(1024)S(1)}, bf16[768,2304]{1,0:T(8,128)(2,1)}, /*index=5*/bf16[2,768]{1,0:T(2,128)(2,1)S(1)}, s32[]{:T(128)}, s32[2,512]{1,0:T(2,128)S(1)}, ...), branch_computations={%region_2.2_spmd, %region_3.21_spmd} | conditional | flops 4853460992 | bytes 64355200 | solution.py:384
  71.4 32.8 %conditional.1 = (f32[512,768]{1,0:T(8,128)S(1)}, f32[512,768]{1,0:T(8,128)}) conditional(s32[]{:T(128)} %clamp.6, (f32[512,768]{1,0:T(8,128)S(1)}, f32[768]{0:T(1024)S(1)}, f32[768]{0:T(1024)S(1)}, bf16[768,2304]{1,0:T(8,128)(2,1)}, bf16[2,768]{1,0:T(2,128)(2,1)S(1)}, /*index=5*/s32[]{:T(128)}, ...), branch_computations={%region_4.7_spmd, %region_9.12_spmd, %region_13.17_spmd, %region_1... | conditional | flops 4851757056 | bytes 57530968
  112.2 13.8 collective-permute-done
  130.0 37.6 %conditional.16 = (bf16[512,768]{1,0:T(8,128)(2,1)}) conditional(s32[]{:T(128)} %convert_element_type.603, () %tuple.214, (s32[]{:T(128)}, bf16[512,768]{1,0:T(8,128)(2,1)}, f32[768]{0:T(1024)S(1)}, f32[768]{0:T(1024)S(1)}, bf16[768,2304]{1,0:T(8,128)(2,1)}, /*index=5*/bf16[2,768]{1,0:T(2,128)(2,1)S(1)}, s32[]{:T(128)}, s32[2,512]{1,0:T(2,128)S(1)}, ...), branch_computations={%region_2.2_spmd, %region_3.21_spmd} | conditional | flops 4853460992 | bytes 64355200 | solution.py:384
  132.4 32.8 %conditional.1 = (f32[512,768]{1,0:T(8,128)S(1)}, f32[512,768]{1,0:T(8,128)}) conditional(s32[]{:T(128)} %clamp.6, (f32[512,768]{1,0:T(8,128)S(1)}, f32[768]{0:T(1024)S(1)}, f32[768]{0:T(1024)S(1)}, bf16[768,2304]{1,0:T(8,128)(2,1)}, bf16[2,768]{1,0:T(2,128)(2,1)S(1)}, /*index=5*/s32[]{:T(128)}, ...), branch_computations={%region_4.7_spmd, %region_9.12_spmd, %region_13.17_spmd, %region_1... | conditional | flops 4851757056 | bytes 57530968
  193.8 40.9 %collective-permute-start = (bf16[512,768]{1,0:T(8,128)(2,1)}, bf16[512,768]{1,0:T(8,128)(2,1)S(1)}, u32[]{:S(2)}, u32[]{:S(2)}) collective-permute-start(bf16[512,768]{1,0:T(8,128)(2,1)} %get-tuple-element.2401), channel_id=1, source_target_pairs={{0,8},{8,16},{16,24},{1,9},{9,17},{17,25},{2,10},{10,18},{18,26},{... | collective-permute-start | bytes 2359304 | tf_op jit(solution)/shard_map/while/body/eval_jaxpr/ppermute | solution.py:27
  280.5 41.7 %collective-permute-start = (bf16[512,768]{1,0:T(8,128)(2,1)}, bf16[512,768]{1,0:T(8,128)(2,1)S(1)}, u32[]{:S(2)}, u32[]{:S(2)}) collective-permute-start(bf16[512,768]{1,0:T(8,128)(2,1)} %get-tuple-element.2401), channel_id=1, source_target_pairs={{0,8},{8,16},{16,24},{1,9},{9,17},{17,25},{2,10},{10,18},{18,26},{... | collective-permute-start | bytes 2359304 | tf_op jit(solution)/shard_map/while/body/eval_jaxpr/ppermute | solution.py:27
  339.1 1207.3 %while.42 = (s32[]{:T(128)}, bf16[512,768]{1,0:T(8,128)(2,1)}, bf16[2,512,768]{2,1,0:T(8,128)(2,1)}, f32[8,1180800]{1,0:T(8,128)}, s32[]{:T(128)}, /*index=5*/s3...) while((s32[]{:T(128)}, bf16[512,768]{1,0:T(8,128)(2,1)}, ...), condition=%wide.region_75.77_spmd.clone, body=%wide.region_24.76_spmd.clone.sunk | while | flops 12183992320 | bytes 571896064 | solution.py:457
  349.3 14.9 conditional.17
  365.5 26.5 %select_add_fusion.2 = f32[8,1180800]{1,0:T(8,128)} fusion(f32[8,1180800]{1,0:T(8,128)} %get-tuple-element.2192, f32[8,1180800]{1,0:T(8,128)} %get-tuple-element.2342, pred[]{:T(512)S(6)} %compare.69), kind=kLoop, calls=%fused_computation.465.clone.1 | loop fusion | flops 18892800 | bytes 113356800 | tf_op jit(solution)/shard_map/while/body/eval_jaxpr/add | solution.py:451
  410.8 37.4 %select_add_fusion.2 = f32[8,1180800]{1,0:T(8,128)} fusion(f32[8,1180800]{1,0:T(8,128)} %get-tuple-element.2192, f32[8,1180800]{1,0:T(8,128)} %get-tuple-element.2342, pred[]{:T(512)S(6)} %compare.69), kind=kLoop, calls=%fused_computation.465.clone.1 | loop fusion | flops 18892800 | bytes 113356800 | tf_op jit(solution)/shard_map/while/body/eval_jaxpr/add | solution.py:451
  467.1 37.4 %select_add_fusion.2 = f32[8,1180800]{1,0:T(8,128)} fusion(f32[8,1180800]{1,0:T(8,128)} %get-tuple-element.2192, f32[8,1180800]{1,0:T(8,128)} %get-tuple-element.2342, pred[]{:T(512)S(6)} %compare.69), kind=kLoop, calls=%fused_computation.465.clone.1 | loop fusion | flops 18892800 | bytes 113356800 | tf_op jit(solution)/shard_map/while/body/eval_jaxpr/add | solution.py:451
  506.3 498.0 %collective-permute-done.1 = bf16[512,768]{1,0:T(8,128)(2,1)} collective-permute-done((bf16[512,768]{1,0:T(8,128)(2,1)}, bf16[512,768]{1,0:T(8,128)(2,1)}, u32[]{:S(2)}, u32[]{:S(2)}) %collective-permute-start.1) | collective-permute-done | bytes 786464 | tf_op jit(solution)/shard_map/while/body/eval_jaxpr/ppermute | solution.py:27
  1005.7 166.3 %conditional.17 = ((bf16[512,768]{1,0:T(8,128)(2,1)}, f32[8,1180800]{1,0:T(8,128)})) conditional(s32[]{:T(128)} %convert_element_type.604, () %tuple.217, (s32[]{:T(128)}, pred[]{:T(512)}, bf16[2,512,768]{2,1,0:T(8,128)(2,1)}, s32[]{:T(128)}, bf16[512,768]{1,0:T(8,128)(2,1)}, /*index=5*/bf16[2,512,768]{2,1,0:T(8,128)(2,1)}, f32[768]{0:T(1024)}, ...), branch_computations={%region_25.26_spmd, %region_26.74_spmd} | conditional | flops 12164313088 | bytes 426122656 | solution.py:447
  1007.9 162.5 %conditional.3 = (bf16[512,768]{1,0:T(8,128)(2,1)}, f32[8,1180800]{1,0:T(8,128)}) conditional(s32[]{:T(128)} %clamp.7, (bf16[512,768]{1,0:T(8,128)(2,1)S(1)}, s32[]{:T(128)}, bf16[2,512,768]{2,1,0:T(8,128)(2,1)S(1)}, f32[768]{0:T(1024)S(1)}, f32[768]{0:T(1024)S(1)}, /*index=5*/bf16[768,2304]{1,0:T(8,128)(2,1)}, ...), branch_computations={%region_27.39_spmd, %region_40.51_spmd, %region_52.64_spmd, %regio... | conditional | flops 12163395584 | bytes 416816000 | solution.py:434
  1086.7 20.4 dynamic-update-slice.32
  1121.5 18.0 pad.20
  1173.4 37.4 %select_add_fusion.2 = f32[8,1180800]{1,0:T(8,128)} fusion(f32[8,1180800]{1,0:T(8,128)} %get-tuple-element.2192, f32[8,1180800]{1,0:T(8,128)} %get-tuple-element.2342, pred[]{:T(512)S(6)} %compare.69), kind=kLoop, calls=%fused_computation.465.clone.1 | loop fusion | flops 18892800 | bytes 113356800 | tf_op jit(solution)/shard_map/while/body/eval_jaxpr/add | solution.py:451
  1213.7 115.2 %collective-permute-done.1 = bf16[512,768]{1,0:T(8,128)(2,1)} collective-permute-done((bf16[512,768]{1,0:T(8,128)(2,1)}, bf16[512,768]{1,0:T(8,128)(2,1)}, u32[]{:S(2)}, u32[]{:S(2)}) %collective-permute-start.1) | collective-permute-done | bytes 786464 | tf_op jit(solution)/shard_map/while/body/eval_jaxpr/ppermute | solution.py:27
  1330.6 166.1 %conditional.17 = ((bf16[512,768]{1,0:T(8,128)(2,1)}, f32[8,1180800]{1,0:T(8,128)})) conditional(s32[]{:T(128)} %convert_element_type.604, () %tuple.217, (s32[]{:T(128)}, pred[]{:T(512)}, bf16[2,512,768]{2,1,0:T(8,128)(2,1)}, s32[]{:T(128)}, bf16[512,768]{1,0:T(8,128)(2,1)}, /*index=5*/bf16[2,512,768]{2,1,0:T(8,128)(2,1)}, f32[768]{0:T(1024)}, ...), branch_computations={%region_25.26_spmd, %region_26.74_spmd} | conditional | flops 12164313088 | bytes 426122656 | solution.py:447
  1332.7 162.4 %conditional.3 = (bf16[512,768]{1,0:T(8,128)(2,1)}, f32[8,1180800]{1,0:T(8,128)}) conditional(s32[]{:T(128)} %clamp.7, (bf16[512,768]{1,0:T(8,128)(2,1)S(1)}, s32[]{:T(128)}, bf16[2,512,768]{2,1,0:T(8,128)(2,1)S(1)}, f32[768]{0:T(1024)S(1)}, f32[768]{0:T(1024)S(1)}, /*index=5*/bf16[768,2304]{1,0:T(8,128)(2,1)}, ...), branch_computations={%region_27.39_spmd, %region_40.51_spmd, %region_52.64_spmd, %regio... | conditional | flops 12163395584 | bytes 416816000 | solution.py:434
  1411.4 20.4 dynamic-update-slice.32
  1446.2 18.0 pad.20
  1498.0 37.4 %select_add_fusion.2 = f32[8,1180800]{1,0:T(8,128)} fusion(f32[8,1180800]{1,0:T(8,128)} %get-tuple-element.2192, f32[8,1180800]{1,0:T(8,128)} %get-tuple-element.2342, pred[]{:T(512)S(6)} %compare.69), kind=kLoop, calls=%fused_computation.465.clone.1 | loop fusion | flops 18892800 | bytes 113356800 | tf_op jit(solution)/shard_map/while/body/eval_jaxpr/add | solution.py:451
  1551.1 721.8 %all-reduce.8.cloned.1.call-done = f32[8,1180800]{1,0:T(8,128)} async-done(((f32[8,1180800]{1,0:T(8,128)}), f32[8,1180800]{1,0:T(8,128)}) %all-reduce.8.cloned.1.call-update) | async-done | bytes 37785616
  2272.8 17.3 fusion.349
  2290.1 74.1 %all-reduce.10.cloned.1.call-done = (bf16[2,512,768]{2,1,0:T(8,128)(2,1)}, bf16[2,512,768]{2,1,0:T(8,128)(2,1)}) async-done(((bf16[2,512,768]{2,1,0:T(8,128)(2,1)}, bf16[2,512,768]{2,1,0:T(8,128)(2,1)}), (bf16[2,512,768]{2,1,0:T(8,128)(2,1)}, bf16[2,512,768]{2,1,0:T(8,128)(2,1)})) %all-reduce.10.cloned.1.call-update) | async-done | bytes 3145744 | tf_op jit(solution)/shard_map/psum | solution.py:32
  2369.9 172.5 %all-gather.3.cloned.1.call-done = bf16[4,1,1180800]{2,1,0:T(2,128)(2,1)} async-done(((bf16[1,1,1180800]{2,1,0:T(2,128)(2,1)}), bf16[4,1,1180800]{2,1,0:T(2,128)(2,1)}) %all-gather.3.cloned.1.call-update) | async-done | bytes 9446416 | tf_op jit(solution)/shard_map/all_gather | solution.py:462
  2542.4 14.0 copy.124
  2568.6 13.8 slice_reduce_fusion.2
  2582.4 27.2 %slice_reduce_fusion = (f32[589824]{0:T(1024)}, f32[589824]{0:T(1024)}) fusion(f32[4,1180800]{1,0:T(4,128)S(1)} %bitcast.452), kind=kLoop, calls=%fused_computation.478 | loop fusion | bytes 9437184 | tf_op jit(solution)/shard_map/slice | solution.py:305
  (581 shorter events, 547.0 us)
Async XLA Ops:
  7.2 2265.7 %all-reduce.8.cloned.1.call-start = ((), (), s32[]{:S(2)}) async-start(), calls=%async_computation.1 | async-start | bytes 75571200
  106.6 19.4 collective-permute-start
  167.6 21.3 collective-permute-start
  193.8 57.1 %copy-start.40 = (bf16[2,3072]{1,0:T(2,128)(2,1)S(1)}, bf16[2,3072]{1,0:T(2,128)(2,1)}, u32[]{:S(2)}) copy-start(bf16[2,3072]{1,0:T(2,128)(2,1)} %copy-done.39) | copy-start | bytes 36868 | tf_op jit(solution)/shard_map/while
  193.8 57.1 %copy-start.62 = (bf16[2,768]{1,0:T(2,128)(2,1)S(1)}, bf16[2,768]{1,0:T(2,128)(2,1)}, u32[]{:S(2)}) copy-start(bf16[2,768]{1,0:T(2,128)(2,1)} %copy-done.61) | copy-start | bytes 9220 | tf_op jit(solution)/shard_map/while
  193.8 57.1 %collective-permute-start = (bf16[512,768]{1,0:T(8,128)(2,1)}, bf16[512,768]{1,0:T(8,128)(2,1)S(1)}, u32[]{:S(2)}, u32[]{:S(2)}) collective-permute-start(bf16[512,768]{1,0:T(8,128)(2,1)} %get-tuple-element.2401), channel_id=1, source_target_pairs={{0,8},{8,16},{16,24},{1,9},{9,17},{17,25},{2,10},{10,18},{18,26},{... | collective-permute-start | bytes 2359304 | tf_op jit(solution)/shard_map/while/body/eval_jaxpr/ppermute | solution.py:27
  255.8 19.8 collective-permute-start
  280.5 56.4 %copy-start.40 = (bf16[2,3072]{1,0:T(2,128)(2,1)S(1)}, bf16[2,3072]{1,0:T(2,128)(2,1)}, u32[]{:S(2)}) copy-start(bf16[2,3072]{1,0:T(2,128)(2,1)} %copy-done.39) | copy-start | bytes 36868 | tf_op jit(solution)/shard_map/while
  280.5 56.4 %copy-start.62 = (bf16[2,768]{1,0:T(2,128)(2,1)S(1)}, bf16[2,768]{1,0:T(2,128)(2,1)}, u32[]{:S(2)}) copy-start(bf16[2,768]{1,0:T(2,128)(2,1)} %copy-done.61) | copy-start | bytes 9220 | tf_op jit(solution)/shard_map/while
  280.5 56.4 %collective-permute-start = (bf16[512,768]{1,0:T(8,128)(2,1)}, bf16[512,768]{1,0:T(8,128)(2,1)S(1)}, u32[]{:S(2)}, u32[]{:S(2)}) collective-permute-start(bf16[512,768]{1,0:T(8,128)(2,1)} %get-tuple-element.2401), channel_id=1, source_target_pairs={{0,8},{8,16},{16,24},{1,9},{9,17},{17,25},{2,10},{10,18},{18,26},{... | collective-permute-start | bytes 2359304 | tf_op jit(solution)/shard_map/while/body/eval_jaxpr/ppermute | solution.py:27
  364.1 29.6 %collective-permute-start.1 = (bf16[512,768]{1,0:T(8,128)(2,1)}, bf16[512,768]{1,0:T(8,128)(2,1)}, u32[]{:S(2)}, u32[]{:S(2)}) collective-permute-start(bf16[512,768]{1,0:T(8,128)(2,1)} %get-tuple-element.2191), channel_id=1, source_target_pairs={{8,0},{16,8},{24,16},{9,1},{17,9},{25,17},{10,2},{18,10},{26,18},{... | collective-permute-start | bytes 2359304 | tf_op jit(solution)/shard_map/while/body/eval_jaxpr/ppermute | solution.py:27
  409.5 40.5 %collective-permute-start.1 = (bf16[512,768]{1,0:T(8,128)(2,1)}, bf16[512,768]{1,0:T(8,128)(2,1)}, u32[]{:S(2)}, u32[]{:S(2)}) collective-permute-start(bf16[512,768]{1,0:T(8,128)(2,1)} %get-tuple-element.2191), channel_id=1, source_target_pairs={{8,0},{16,8},{24,16},{9,1},{17,9},{25,17},{10,2},{18,10},{26,18},{... | collective-permute-start | bytes 2359304 | tf_op jit(solution)/shard_map/while/body/eval_jaxpr/ppermute | solution.py:27
  410.8 38.2 %copy-start.17 = (bf16[2,512,768]{2,1,0:T(8,128)(2,1)S(1)}, bf16[2,512,768]{2,1,0:T(8,128)(2,1)}, u32[]{:S(2)}) copy-start(bf16[2,512,768]{2,1,0:T(8,128)(2,1)} %get-tuple-element.2341) | copy-start | bytes 4718596 | tf_op jit(solution)/shard_map/while
  465.8 538.5 %collective-permute-start.1 = (bf16[512,768]{1,0:T(8,128)(2,1)}, bf16[512,768]{1,0:T(8,128)(2,1)}, u32[]{:S(2)}, u32[]{:S(2)}) collective-permute-start(bf16[512,768]{1,0:T(8,128)(2,1)} %get-tuple-element.2191), channel_id=1, source_target_pairs={{8,0},{16,8},{24,16},{9,1},{17,9},{25,17},{10,2},{18,10},{26,18},{... | collective-permute-start | bytes 2359304 | tf_op jit(solution)/shard_map/while/body/eval_jaxpr/ppermute | solution.py:27
  504.6 499.8 %copy-start.1 = (bf16[2,512,768]{2,1,0:T(8,128)(2,1)S(1)}, bf16[2,512,768]{2,1,0:T(8,128)(2,1)}, u32[]{:S(2)}) copy-start(bf16[2,512,768]{2,1,0:T(8,128)(2,1)} %copy-done) | copy-start | bytes 4718596 | tf_op jit(solution)/shard_map/while
  504.6 499.8 %copy-start.24 = (f32[768]{0:T(1024)S(1)}, f32[768]{0:T(1024)}, u32[]{:S(2)}) copy-start(f32[768]{0:T(1024)} %copy-done.23) | copy-start | bytes 9220 | tf_op jit(solution)/shard_map/while
  504.6 499.8 %copy-start.36 = (f32[768]{0:T(1024)S(1)}, f32[768]{0:T(1024)}, u32[]{:S(2)}) copy-start(f32[768]{0:T(1024)} %copy-done.35) | copy-start | bytes 9220 | tf_op jit(solution)/shard_map/while
  504.6 499.8 %copy-start.42 = (bf16[2,3072]{1,0:T(2,128)(2,1)S(1)}, bf16[2,3072]{1,0:T(2,128)(2,1)}, u32[]{:S(2)}) copy-start(bf16[2,3072]{1,0:T(2,128)(2,1)} %copy-done.41) | copy-start | bytes 36868 | tf_op jit(solution)/shard_map/while
  504.6 499.8 %copy-start.54 = (bf16[2,768]{1,0:T(2,128)(2,1)S(1)}, bf16[2,768]{1,0:T(2,128)(2,1)}, u32[]{:S(2)}) copy-start(bf16[2,768]{1,0:T(2,128)(2,1)} %copy-done.53) | copy-start | bytes 9220 | tf_op jit(solution)/shard_map/while
  504.6 499.8 %copy-start.72 = (s32[2]{0:T(128)S(1)}, s32[2]{0:T(128)}, u32[]{:S(2)}) copy-start(s32[2]{0:T(128)} %copy-done.71) | copy-start | bytes 28 | tf_op jit(solution)/shard_map/while
  506.3 498.0 %copy-start.18 = (bf16[2,512,768]{2,1,0:T(8,128)(2,1)}, bf16[2,512,768]{2,1,0:T(8,128)(2,1)S(1)}, u32[]{:S(2)}) copy-start(bf16[2,512,768]{2,1,0:T(8,128)(2,1)S(1)} %fusion.433) | copy-start | bytes 4718596 | tf_op jit(solution)/shard_map/while
  1172.1 156.8 %collective-permute-start.1 = (bf16[512,768]{1,0:T(8,128)(2,1)}, bf16[512,768]{1,0:T(8,128)(2,1)}, u32[]{:S(2)}, u32[]{:S(2)}) collective-permute-start(bf16[512,768]{1,0:T(8,128)(2,1)} %get-tuple-element.2191), channel_id=1, source_target_pairs={{8,0},{16,8},{24,16},{9,1},{17,9},{25,17},{10,2},{18,10},{26,18},{... | collective-permute-start | bytes 2359304 | tf_op jit(solution)/shard_map/while/body/eval_jaxpr/ppermute | solution.py:27
  1210.8 118.0 %copy-start.1 = (bf16[2,512,768]{2,1,0:T(8,128)(2,1)S(1)}, bf16[2,512,768]{2,1,0:T(8,128)(2,1)}, u32[]{:S(2)}) copy-start(bf16[2,512,768]{2,1,0:T(8,128)(2,1)} %copy-done) | copy-start | bytes 4718596 | tf_op jit(solution)/shard_map/while
  1210.8 118.0 %copy-start.24 = (f32[768]{0:T(1024)S(1)}, f32[768]{0:T(1024)}, u32[]{:S(2)}) copy-start(f32[768]{0:T(1024)} %copy-done.23) | copy-start | bytes 9220 | tf_op jit(solution)/shard_map/while
  1210.8 118.0 %copy-start.36 = (f32[768]{0:T(1024)S(1)}, f32[768]{0:T(1024)}, u32[]{:S(2)}) copy-start(f32[768]{0:T(1024)} %copy-done.35) | copy-start | bytes 9220 | tf_op jit(solution)/shard_map/while
  1210.8 118.0 %copy-start.42 = (bf16[2,3072]{1,0:T(2,128)(2,1)S(1)}, bf16[2,3072]{1,0:T(2,128)(2,1)}, u32[]{:S(2)}) copy-start(bf16[2,3072]{1,0:T(2,128)(2,1)} %copy-done.41) | copy-start | bytes 36868 | tf_op jit(solution)/shard_map/while
  1210.8 118.0 %copy-start.54 = (bf16[2,768]{1,0:T(2,128)(2,1)S(1)}, bf16[2,768]{1,0:T(2,128)(2,1)}, u32[]{:S(2)}) copy-start(bf16[2,768]{1,0:T(2,128)(2,1)} %copy-done.53) | copy-start | bytes 9220 | tf_op jit(solution)/shard_map/while
  1210.8 118.0 %copy-start.72 = (s32[2]{0:T(128)S(1)}, s32[2]{0:T(128)}, u32[]{:S(2)}) copy-start(s32[2]{0:T(128)} %copy-done.71) | copy-start | bytes 28 | tf_op jit(solution)/shard_map/while
  1213.7 115.2 %copy-start.18 = (bf16[2,512,768]{2,1,0:T(8,128)(2,1)}, bf16[2,512,768]{2,1,0:T(8,128)(2,1)S(1)}, u32[]{:S(2)}) copy-start(bf16[2,512,768]{2,1,0:T(8,128)(2,1)S(1)} %fusion.433) | copy-start | bytes 4718596 | tf_op jit(solution)/shard_map/while
  1496.7 41.6 %collective-permute-start.1 = (bf16[512,768]{1,0:T(8,128)(2,1)}, bf16[512,768]{1,0:T(8,128)(2,1)}, u32[]{:S(2)}, u32[]{:S(2)}) collective-permute-start(bf16[512,768]{1,0:T(8,128)(2,1)} %get-tuple-element.2191), channel_id=1, source_target_pairs={{8,0},{16,8},{24,16},{9,1},{17,9},{25,17},{10,2},{18,10},{26,18},{... | collective-permute-start | bytes 2359304 | tf_op jit(solution)/shard_map/while/body/eval_jaxpr/ppermute | solution.py:27
  1546.5 817.7 %all-reduce.10.cloned.1.call-start = ((), (), s32[]{:S(2)}) async-start(), calls=%async_computation.2 | async-start | bytes 6291456 | tf_op jit(solution)/shard_map/psum | solution.py:32
  1550.4 992.0 %all-gather.3.cloned.1.call-start = ((), (), s32[]{:S(2)}) async-start(), calls=%async_computation | async-start | bytes 23616000 | tf_op jit(solution)/shard_map/all_gather | solution.py:462
  (140 other events, 906.4 us)
Sparse Core Ops, SparseCore 0:
  1546.6 726.1 all-reduce.7
  2277.1 87.1 all-reduce.9
  2366.2 176.0 all-gather.2
where the time goes:
time: 2650 us; the launch traced here: 2640 us
  waiting for transfers between devices  1650 us (62%)
  local copies, waits for them, and re-layouts  347 us (13%)
  other arithmetic  269 us (10%)
  matrix products  161 us (6%)
  loops' own time  108 us (4%)
  starting transfers between devices  99.3 us (4%)
    unnamed x4, waiting for transfers between devices  722 us
    ppermute x10, waiting for transfers between devices, shifted_2(): lax.ppermute(value, axis, [(source, source + steps) for source in range(l...  677 us
    add x5, other arithmetic, backward_tick(): totals = totals + flat_terms  176 us
    all_gather x1, waiting for transfers between devices, per_device(): lax.all_gather(shares.astype(jnp.bfloat16), 'segment', axis=0, tiled=True)  172 us
    ppermute x10, starting transfers between devices, shifted_2(): lax.ppermute(value, axis, [(source, source + steps) for source in range(l...  99.1 us
    psum x1, waiting for transfers between devices, spread_2(): return lax.psum(jnp.where(mine, value, jnp.zeros_like(value)), axis)  74.1 us
    another operation x2, loops' own time, backward_compute(): lax.switch(segment_place, [partial(backward_branch, section) for section...  62.1 us
    cond x90, local copies, waits for them, and re-layouts  55 us
  transfers between devices with their start and end apart: 13, of which 10 were waited for; matrix products, arithmetic and copies ran while one was open for 9% of the time, Pallas kernels for 0%

commit v1 on v0

--- a/solution.py
+++ b/solution.py
@@ -4,6 +4,8 @@
 import jax
 import jax.numpy as jnp
 from jax import lax
+from jax.experimental import pallas as pl
+from jax.experimental.pallas import tpu as pltpu
 from jax.sharding import PartitionSpec as P
 
 D = 768
@@ -497,9 +499,594 @@
     )
 
 
+F32 = jnp.float32
+BF16 = jnp.bfloat16
+MESH = pl.DeviceIdType.MESH
+MIB = 2**20
+
+
+def mm(a, b):
+    return lax.dot_general(a, b, (((1,), (0,)), ((), ())), preferred_element_type=F32)
+
+
+def mm_t(a, b):
+    return lax.dot_general(a, b, (((1,), (1,)), ((), ())), preferred_element_type=F32)
+
+
+def ln_parts(h):
+    center = h - jnp.mean(h, axis=-1, keepdims=True)
+    r = lax.rsqrt(jnp.mean(center * center, axis=-1, keepdims=True) + 1e-05)
+    return center * r, r
+
+
+def gelu_both(x):
+    x2 = x * x
+    t = jnp.tanh(0.7978845608028654 * (x + 0.044715 * x2 * x))
+    half = 0.5 * (1.0 + t)
+    slope = half + (0.5 * x) * (1.0 - t * t) * (
+        0.7978845608028654 + (3.0 * 0.044715 * 0.7978845608028654) * x2
+    )
+    return x * half, slope
+
+
+def places():
+    seg = lax.axis_index("segment")
+    dp = lax.axis_index("dp")
+    return seg, dp, dp // 2, dp % 2, seg // 2, seg % 2
+
+
+def chain_kernel(
+    tok, cot, oh, gb, sm, ub, wq_h, wo_h, wu_h, wd_h,
+    x1o, x3o, g2o, c4o, pao, comb, smo,
+    wq, wo, wu, wd, hbuf, xa, proj, kvo, ctx, prob, bias, xf1, xf3, act, acts, dg1, dg1s, dg3,
+    gbuf, cg, pga, dks, dkr, lt, pb, dxs, full, pieces, gball, ohv,
+    w_sem, in_sem, gs_sem, gr_sem, ts_sem, tr_sem, c_sem, cs_sem, cr_sem, kvs_sem, kvr_sem,
+    dks_sem, dkr_sem, as_sem, ar_sem, al_sem, pb_sem, fs_sem, fr_sem, us_sem, ur_sem, g4_sem,
+):
+    seg, dp, z, k, y, x = places()
+    other = 1 - k
+    partner = (seg, 2 * z + other)
+
+    def peer(d):
+        return ((seg + d) % 4, dp)
+
+    def back(d):
+        return (seg + 4 - d) % 4
+
+    loads = {}
+
+    def load(name, src, dst, sem):
+        copy = pltpu.make_async_copy(src, dst, sem)
+        copy.start()
+        loads[name] = copy
+
+    load("q0", wq_h.at[0], wq.at[0], w_sem.at[0])
+    load("o0", wo_h.at[0], wo.at[0], w_sem.at[1])
+
+    barrier = pltpu.get_barrier_semaphore()
+    for d in range(4):
+        for c in range(2):
+            if d == 0 and c == 1:
+                continue
+            where = partner if d == 0 else ((seg + d) % 4, 2 * z + c)
+            pl.semaphore_signal(barrier, inc=1, device_id=where, device_id_type=MESH)
+    pl.semaphore_wait(barrier, 7)
+
+    def remote(src, dst, ssem, rsem, where):
+        return pltpu.make_async_remote_copy(
+            src_ref=src, dst_ref=dst, send_sem=ssem, recv_sem=rsem,
+            device_id=where, device_id_type=MESH,
+        )
+
+    own_tok = pl.ds(pl.multiple_of(256 * k, 256), 256)
+    far_tok = pl.ds(pl.multiple_of(256 * other, 256), 256)
+    tok_here = pltpu.make_async_copy(tok.at[x, own_tok], hbuf.at[0], in_sem.at[0])
+    oh_here = pltpu.make_async_copy(oh.at[x], ohv, in_sem.at[1])
+    tok_far = remote(tok.at[x, far_tok], hbuf.at[0], ts_sem.at[0], tr_sem.at[0], partner)
+    oh_far = remote(oh.at[x], ohv, ts_sem.at[1], tr_sem.at[1], partner)
+
+    @pl.when(k == y)
+    def _():
+        tok_here.start()
+        oh_here.start()
+        tok_far.start()
+        oh_far.start()
+
+    gains = [
+        remote(gb, gball.at[seg], gs_sem.at[d - 1], gr_sem.at[d - 1], peer(d)) for d in (1, 2, 3)
+    ]
+    for copy in gains:
+        copy.start()
+    load("u0", wu_h.at[0], wu.at[0], w_sem.at[2])
+    load("u1", wu_h.at[1], wu.at[1], w_sem.at[3])
+    load("d0", wd_h.at[0], wd.at[0], w_sem.at[4])
+    load("d1", wd_h.at[1], wd.at[1], w_sem.at[5])
+    cots = []
+    for m in range(2):
+        here = pltpu.make_async_copy(cot.at[m, own_tok], c4o.at[2 * k + m], c_sem.at[m])
+        there = remote(
+            cot.at[m, far_tok], c4o.at[2 * k + m], cs_sem.at[m], cr_sem.at[m], partner
+        )
+        here.start()
+        there.start()
+        cots.append((here, there))
+    load("q1", wq_h.at[1], wq.at[1], w_sem.at[6])
+    load("o1", wo_h.at[1], wo.at[1], w_sem.at[7])
+
+    gball[seg] = gb[...]
+    smo[...] = jnp.zeros_like(smo)
+    for copy in gains:
+        copy.wait()
+
+    @pl.when(k == y)
+    def _():
+        tok_here.wait()
+        oh_here.wait()
+        tok_far.wait_send()
+        oh_far.wait_send()
+
+    @pl.when(k != y)
+    def _():
+        tok_far.wait_recv()
+        oh_far.wait_recv()
+
+    group_lane = (lax.broadcasted_iota(jnp.int32, (256, 128), 1) < 3).astype(F32).astype(BF16)
+    mine = ohv[own_tok, :] * group_lane
+    theirs = ohv[far_tok, :]
+    same = mm_t(jnp.concatenate([ohv[own_tok, :], theirs], axis=0), mine)
+    bias[...] = jnp.where(same > 0.5, 0.0, -1e30)
+
+    lane = lax.broadcasted_iota(jnp.int32, (1, 128), 1)
+    head_mask = [(lane < 64).astype(F32).astype(BF16), (lane >= 64).astype(F32).astype(BF16)]
+    head_scaled = [part * 0.125 for part in head_mask]
+
+    def gain_of(s):
+        return gball[s, 0:1, :], gball[s, 1:2, :]
+
+    def normed(s):
+        n, _ = ln_parts(hbuf[s].astype(F32))
+        gain, shift = gain_of(s)
+        return (n * gain + shift).astype(BF16)
+
+    def lanes(start, width):
+        return pl.ds(pl.multiple_of(start, 128), width)
+
+    def attn_fwd(l):
+        s = 2 * l
+        xin = normed(s)
+        xa[l] = xin
+        loads[f"q{l}"].wait()
+        kv = remote(
+            proj.at[l, :, pl.ds(768, 1536)], kvo.at[l], kvs_sem.at[l], kvr_sem.at[l], partner
+        )
+        for n in (1, 2, 0):
+            part = mm(xin, wq[l, :, 768 * n : 768 * (n + 1)])
+            if n != 1:
+                row = 2 * l + (n == 2)
+                part = part + sm[row : row + 1, :]
+            proj[l, :, 768 * n : 768 * (n + 1)] = part.astype(BF16)
+            if n == 2:
+                kv.start()
+        kv.wait()
+
+        def pair(hp, carry):
+            lo = hp * 128
+            q = proj[l, :, lanes(lo, 128)]
+            kk = jnp.concatenate([proj[l, :, lanes(768 + lo, 128)], kvo[l, :, lanes(lo, 128)]], 0)
+            vv = jnp.concatenate(
+                [proj[l, :, lanes(1536 + lo, 128)], kvo[l, :, lanes(768 + lo, 128)]], 0
+            )
+            vt = vv.T
+            outs = []
+            for j in range(2):
+                st = mm_t(kk, q * head_scaled[j]) + bias[...]
+                e = jnp.exp(st - jnp.max(st, axis=0, keepdims=True))
+                p = (e * (1.0 / jnp.sum(e, axis=0, keepdims=True))).astype(BF16)
+                prob[l, 2 * hp + j] = p
+                outs.append(mm(vt[64 * j : 64 * (j + 1)], p))
+            ctx[l, :, lanes(lo, 128)] = jnp.concatenate(outs, 0).T.astype(BF16)
+            return carry
+
+        lax.fori_loop(0, 6, pair, 0)
+        loads[f"o{l}"].wait()
+        out = mm(ctx[l], wo[l]) + sm[4 + l : 5 + l, :]
+        hbuf[s + 1] = (hbuf[s].astype(F32) + out).astype(BF16)
+
+    def ffn_up(rows_in, slot, e, act_ref, dg_ref):
+        def step(n, carry):
+            at = lanes(256 * n, 256)
+            pre = mm(rows_in, wu[slot, :, at]) + ub[12 * e + n]
+            a, slope = gelu_both(pre)
+            act_ref[:, at] = a.astype(BF16)
+            dg_ref[:, at] = slope.astype(BF16)
+            return carry
+
+        lax.fori_loop(0, 12, step, 0)
+
+    def ffn_down(act_ref, slot, e):
+        return mm(act_ref[...], wd[slot]) + sm[pl.ds(8 + e, 1), :]
+
+    row = lax.broadcasted_iota(jnp.int32, (256, 1), 0)
+    is_first = ((row < PATCHES) | (k == 1)).astype(F32)
+    is_second = ((row >= PATCHES) & (k == 0)).astype(F32)
+
+    def push_all(src, dst, slot):
+        local = pltpu.make_async_copy(src, dst.at[seg], al_sem.at[slot])
+        local.start()
+        copies = [
+            remote(src, dst.at[seg], as_sem.at[slot, d - 1], ar_sem.at[slot, d - 1], peer(d))
+            for d in (1, 2, 3)
+        ]
+        for copy in copies:
+            copy.start()
+        return local, copies
+
+    attn_fwd(0)
+
+    xf1[...] = normed(1)
+    sent1 = push_all(xf1, x1o, 0)
+    loads["u0"].wait()
+    loads["u1"].wait()
+    ffn_up(xf1[...], k, k, act, dg1)
+    ffn_up(xf1[192:256, :], 1, 1, acts, dg1s)
+    loads["d0"].wait()
+    loads["d1"].wait()
+    dxs[...] = ffn_down(act, k, k)
+    second = ffn_down(acts, 1, 1)
+    m2 = is_second[192:256]
+    dxs[192:256, :] = jnp.where(m2 > 0.5, second, dxs[192:256, :])
+    hbuf[2] = (hbuf[1].astype(F32) + dxs[...]).astype(BF16)
+    load("u2", wu_h.at[2], wu.at[0], w_sem.at[8])
+    load("d2", wd_h.at[2], wd.at[0], w_sem.at[9])
+
+    attn_fwd(1)
+
+    xf3[...] = normed(3)
+    sent3 = push_all(xf3, x3o, 1)
+    loads["u2"].wait()
+    ffn_up(xf3[...], 0, 2, act, dg3)
+    loads["d2"].wait()
+    for m in range(2):
+        cots[m][0].wait()
+        cots[m][1].wait()
+    g4 = pltpu.make_async_copy(c4o.at[seg], gbuf.at[3], g4_sem)
+    g4.start()
+    h4 = (hbuf[3].astype(F32) + ffn_down(act, 0, 2)).astype(BF16)
+    hbuf[4] = h4
+    g4.wait()
+
+    def ffn_back(g, slot, e, act_ref, dg_ref):
+        def step(n, carry):
+            at = lanes(256 * n, 256)
+            ag = mm_t(g, wd[slot, pl.ds(pl.multiple_of(256 * n, 256), 256), :])
+            pg = (ag * dg_ref[:, at].astype(F32)).astype(BF16)
+            act_ref[:, at] = pg
+            spot = (pl.ds(14 + 4 * e + n // 3, 1), lanes(256 * (n % 3), 256))
+            smo[spot] = smo[spot] + jnp.sum(pg.astype(F32), axis=0, keepdims=True)
+            return carry
+
+        lax.fori_loop(0, 12, step, 0)
+        return mm_t(act_ref[...], wu[slot])
+
+    def norm_back(s, g):
+        n, r = ln_parts(hbuf[s].astype(F32))
+        gain, _ = gain_of(s)
+        dx = dxs[...]
+        smo[s : s + 1, :] = jnp.sum(dx * n, axis=0, keepdims=True)
+        smo[4 + s : 5 + s, :] = jnp.sum(dx, axis=0, keepdims=True)
+        c = dx * gain
+        return g.astype(F32) + r * (
+            c - jnp.mean(c, axis=-1, keepdims=True) - n * jnp.mean(c * n, axis=-1, keepdims=True)
+        )
+
+    g = gbuf[3]
+    smo[28:29, :] = jnp.sum(g.astype(F32), axis=0, keepdims=True)
+    dxs[...] = ffn_back(g, 0, 2, act, dg3)
+    load("u3", wu_h.at[0], wu.at[0], w_sem.at[2])
+    load("d3", wd_h.at[0], wd.at[0], w_sem.at[4])
+    gbuf[2] = norm_back(3, g).astype(BF16)
+
+    pb_copies = []
+
+    def attn_back(l):
+        s = 2 * l
+        g = gbuf[s]
+        smo[12 + l : 13 + l, :] = jnp.sum(g.astype(F32), axis=0, keepdims=True)
+        cg[...] = mm_t(g, wo[l]).astype(BF16)
+
+        def pair(hp, carry):
+            lo = hp * 128
+            q = proj[l, :, lanes(lo, 128)]
+            kk = jnp.concatenate([proj[l, :, lanes(768 + lo, 128)], kvo[l, :, lanes(lo, 128)]], 0)
+            vv = jnp.concatenate(
+                [proj[l, :, lanes(1536 + lo, 128)], kvo[l, :, lanes(768 + lo, 128)]], 0
+            )
+            kt = kk.T
+            c = cg[:, lanes(lo, 128)]
+            dqs = []
+            dv = jnp.zeros((512, 128), F32)
+            dk = jnp.zeros((512, 128), F32)
+            for j in range(2):
+                p = prob[l, 2 * hp + j]
+                cj = c * head_mask[j]
+                at = mm_t(vv, cj)
+                pf = p.astype(F32)
+                ds = (pf * (at - jnp.sum(at * pf, axis=0, keepdims=True))).astype(BF16)
+                dv = dv + mm(p, cj)
+                dk = dk + mm(ds, q * head_scaled[j])
+                dqs.append(mm(kt[64 * j : 64 * (j + 1)], ds))
+            pga[:, lanes(lo, 128)] = (jnp.concatenate(dqs, 0).T * 0.125).astype(BF16)
+            pga[:, lanes(768 + lo, 128)] = dk[:256].astype(BF16)
+            pga[:, lanes(1536 + lo, 128)] = dv[:256].astype(BF16)
+            dks[:, lanes(lo, 128)] = dk[256:].astype(BF16)
+            dks[:, lanes(768 + lo, 128)] = dv[256:].astype(BF16)
+            return carry
+
+        lax.fori_loop(0, 6, pair, 0)
+        exchange = remote(dks, dkr.at[l], dks_sem.at[l], dkr_sem.at[l], partner)
+        exchange.start()
+        lt[0] = xa[l].T
+        lt[1] = ctx[l].T
+        exchange.wait()
+        pga[:, 768:] = (pga[:, 768:].astype(F32) + dkr[l].astype(F32)).astype(BF16)
+        smo[8 + 2 * l : 9 + 2 * l, :] = jnp.sum(pga[:, :768].astype(F32), axis=0, keepdims=True)
+        smo[9 + 2 * l : 10 + 2 * l, :] = jnp.sum(pga[:, 1536:].astype(F32), axis=0, keepdims=True)
+        dxs[...] = mm_t(pga[...], wq[l])
+        hg = norm_back(s, g)
+
+        def grads():
+            for n in range(4):
+                slot = n % 2
+                if len(pb_copies) >= 2:
+                    pb_copies[-2].wait()
+
+                def step(i, carry):
+                    if n < 3:
+                        out = mm(lt[0], pga[:, lanes(768 * n + 256 * i, 256)])
+                    else:
+                        out = mm(lt[1], gbuf[s, :, lanes(256 * i, 256)])
+                    pb[slot, :, :, lanes(256 * i, 256)] = out.astype(BF16).reshape(8, 96, 256)
+                    return carry
+
+                lax.fori_loop(0, 3, step, 0)
+                copy = pltpu.make_async_copy(
+                    pb.at[slot], pao.at[l, :, :, pl.ds(768 * n, 768)], pb_sem.at[slot]
+                )
+                copy.start()
+                pb_copies.append(copy)
+
+        return hg, grads
+
+    hg, grads = attn_back(1)
+    gbuf[1] = hg.astype(BF16)
+    sent2 = push_all(gbuf.at[1], g2o, 2)
+    grads()
+
+    g = gbuf[1].astype(F32)
+    g_first = (g * is_first).astype(BF16)
+    g_second = (g[192:256] * is_second[192:256]).astype(BF16)
+    sum_first = jnp.sum(g_first.astype(F32), axis=0, keepdims=True)
+    sum_second = jnp.sum(g_second.astype(F32), axis=0, keepdims=True)
+    smo[26:27, :] = jnp.where(k == 0, sum_first, 0.0)
+    smo[27:28, :] = jnp.where(k == 0, sum_second, sum_first)
+    loads["u3"].wait()
+    loads["d3"].wait()
+    dxs[...] = ffn_back(g_first, k, k, act, dg1)
+    dxs[192:256, :] = dxs[192:256, :] + ffn_back(g_second, 1, 1, acts, dg1s)
+    gbuf[0] = norm_back(1, gbuf[1]).astype(BF16)
+
+    hg, grads = attn_back(0)
+    hbuf[0] = hg.astype(BF16)
+    fsend_a = remote(hbuf.at[4], full.at[k], fs_sem, fr_sem, partner)
+    fsend_b = remote(hbuf.at[0], full.at[k], fs_sem, fr_sem, partner)
+
+    @pl.when(k == 1)
+    def _():
+        fsend_a.start()
+        full[1] = hbuf[0]
+
+    @pl.when(k == 0)
+    def _():
+        fsend_b.start()
+        full[0] = hbuf[4]
+
+    grads()
+    fsend_a.wait()
+
+    spot = lax.broadcasted_iota(jnp.int32, (128, 128), 0)
+    col = lax.broadcasted_iota(jnp.int32, (128, 128), 1)
+    everything = full[...].reshape(512, 768)
+    for d in range(4):
+        target = (seg + d) % 4
+        at = spot + 128 * target
+        code = ((col == 16 + at // 32) | (col == 32 + at % 32)).astype(F32).astype(BF16)
+        pick = (mm_t(code, ohv[...]) > 1.5).astype(F32).astype(BF16)
+        pieces[d] = mm(pick, everything).astype(BF16)
+        if d > 0:
+            remote(
+                pieces.at[d], comb.at[k, x], us_sem.at[d], ur_sem.at[k, x], (target, 2 * z + y)
+            ).start()
+        else:
+            far = remote(pieces.at[0], comb.at[k, x], us_sem.at[0], ur_sem.at[k, x], partner)
+            near = pltpu.make_async_copy(pieces.at[0], comb.at[k, x], us_sem.at[0])
+
+            @pl.when(k == y)
+            def _():
+                near.start()
+
+            @pl.when(k != y)
+            def _():
+                far.start()
+
+    for d in range(4):
+        if d > 0:
+            remote(
+                pieces.at[d], comb.at[k, x], us_sem.at[d], ur_sem.at[k, x], partner
+            ).wait_send()
+        else:
+            @pl.when(k == y)
+            def _():
+                near.wait()
+
+            @pl.when(k != y)
+            def _():
+                far.wait_send()
+
+    for j in range(2):
+        for m in range(2):
+            @pl.when(jnp.logical_not((2 * k + m == seg) & (j == k)))
+            def _():
+                remote(
+                    pieces.at[0], comb.at[j, m], us_sem.at[0], ur_sem.at[j, m], partner
+                ).wait_recv()
+
+    for local, copies in (sent1, sent3, sent2):
+        local.wait()
+        for copy in copies:
+            copy.wait()
+    for copy in pb_copies[-2:]:
+        copy.wait()
+
+
+def run_chain(tok, cot, oh, gb, sm, ub, wq, wo, wu, wd):
+    any_ = pl.BlockSpec(memory_space=pl.ANY)
+    vm = pl.BlockSpec(memory_space=pltpu.VMEM)
+    dma = pltpu.SemaphoreType.DMA
+    shape = jax.ShapeDtypeStruct
+    return pl.pallas_call(
+        chain_kernel,
+        out_shape=(
+            shape((4, 256, 768), BF16),
+            shape((4, 256, 768), BF16),
+            shape((4, 256, 768), BF16),
+            shape((4, 256, 768), BF16),
+            shape((2, 8, 96, 3072), BF16),
+            shape((2, 2, 128, 768), BF16),
+            shape((32, 768), F32),
+        ),
+        in_specs=[any_, any_, any_, vm, vm, vm, any_, any_, any_, any_],
+        out_specs=(any_, any_, any_, any_, any_, any_, vm),
+        scratch_shapes=[
+            pltpu.VMEM((2, 768, 2304), BF16),
+            pltpu.VMEM((2, 768, 768), BF16),
+            pltpu.VMEM((2, 768, 3072), BF16),
+            pltpu.VMEM((2, 3072, 768), BF16),
+            pltpu.VMEM((5, 256, 768), BF16),
+            pltpu.VMEM((2, 256, 768), BF16),
+            pltpu.VMEM((2, 256, 2304), BF16),
+            pltpu.VMEM((2, 256, 1536), BF16),
+            pltpu.VMEM((2, 256, 768), BF16),
+            pltpu.VMEM((2, 12, 512, 256), BF16),
+            pltpu.VMEM((512, 256), F32),
+            pltpu.VMEM((256, 768), BF16),
+            pltpu.VMEM((256, 768), BF16),
+            pltpu.VMEM((256, 3072), BF16),
+            pltpu.VMEM((64, 3072), BF16),
+            pltpu.VMEM((256, 3072), BF16),
+            pltpu.VMEM((64, 3072), BF16),
+            pltpu.VMEM((256, 3072), BF16),
+            pltpu.VMEM((4, 256, 768), BF16),
+            pltpu.VMEM((256, 768), BF16),
+            pltpu.VMEM((256, 2304), BF16),
+            pltpu.VMEM((256, 1536), BF16),
+            pltpu.VMEM((2, 256, 1536), BF16),
+            pltpu.VMEM((2, 768, 256), BF16),
+            pltpu.VMEM((2, 8, 96, 768), BF16),
+            pltpu.VMEM((256, 768), F32),
+            pltpu.VMEM((2, 256, 768), BF16),
+            pltpu.VMEM((4, 128, 768), BF16),
+            pltpu.VMEM((4, 8, 768), F32),
+            pltpu.VMEM((512, 128), BF16),
+            dma((10,)), dma((2,)), dma((3,)), dma((3,)), dma((2,)), dma((2,)),
+            dma((2,)), dma((2,)), dma((2,)), dma((2,)), dma((2,)),
+            dma((2,)), dma((2,)), dma((3, 3)), dma((3, 3)), dma((3,)), dma((2,)),
+            dma(()), dma(()), dma((4,)), dma((2, 2)), dma(()),
+        ],
+        compiler_params=pltpu.CompilerParams(
+            collective_id=0, has_side_effects=True, vmem_limit_bytes=62 * MIB
+        ),
+    )(tok, cot, oh, gb, sm, ub, wq, wo, wu, wd)
+
+
+def rolled_inputs(tokens, group_ids, type_ids, out_cotangent):
+    rows = tokens.shape[1]
+    spots = jnp.arange(rows, dtype=jnp.int32)
+    starts = jnp.min(jnp.where(type_ids == 0, spots[None, :], rows), axis=1)
+    tok, cot, oh = [], [], []
+    lanes_at = jnp.arange(128, dtype=jnp.int32)[None, :]
+    for m in range(tokens.shape[0]):
+        s = starts[m]
+        turn = lambda v: lax.dynamic_slice_in_dim(jnp.concatenate([v, v], 0), s, rows, 0)
+        tok.append(turn(tokens[m]))
+        cot.append(turn(out_cotangent[m]))
+        gid = turn(group_ids[m])[:, None]
+        spot = ((spots + s) % rows)[:, None]
+        oh.append(
+            (lanes_at == gid) | (lanes_at == 16 + spot // 32) | (lanes_at == 32 + spot % 32)
+        )
+    return jnp.stack(tok), jnp.stack(cot), jnp.stack(oh).astype(BF16)
+
+
+def fast_device(
+    tokens, group_ids, type_ids, norm_gain, norm_bias, qkv_weight, qv_bias, out_weight,
+    out_bias, up_weight, up_bias, down_weight, down_bias, out_cotangent,
+):
+    seg = lax.axis_index("segment")
+    dp = lax.axis_index("dp")
+    tok, cot, oh = rolled_inputs(tokens, group_ids, type_ids, out_cotangent)
+    gb = jnp.concatenate([norm_gain, norm_bias, jnp.zeros((6, D), BF16)], 0).astype(F32)
+    sm = jnp.concatenate(
+        [qv_bias.reshape(4, D), out_bias, jnp.zeros((2, D), BF16), down_bias,
+         jnp.zeros((5, D), BF16)], 0
+    ).astype(F32)
+    ub = up_bias.astype(F32).reshape(36, 1, 256)
+    x1, x3, g2, c4, pa, comb, smo = run_chain(
+        tok, cot, oh, gb, sm, ub, qkv_weight, out_weight, up_weight, down_weight
+    )
+    k = dp % 2
+    us = lax.dynamic_slice_in_dim(up_weight, seg * 768, 768, 2)
+    ds = lax.dynamic_slice_in_dim(down_weight, seg * 768, 768, 1)
+    bs = lax.dynamic_slice_in_dim(up_bias, seg * 768, 768, 1).astype(F32)
+    img = (jnp.arange(256)[None, :] < PATCHES) & (k == 0)
+    img = jnp.broadcast_to(img, (4, 256)).reshape(1024)
+    ups, downs = [], []
+    for e in range(3):
+        xs = (x3 if e == 2 else x1).reshape(1024, 768)
+        gs = (c4 if e == 2 else g2).reshape(1024, 768)
+        if e < 2:
+            gs = jnp.where((img == (e == 0))[:, None], gs, 0)
+        a, slope = gelu_both(mm(xs, us[e]) + bs[e])
+        pg = (mm_t(gs, ds[e]) * slope).astype(BF16)
+        ups.append(mm(xs.T, pg))
+        downs.append(mm(a.astype(BF16).T, gs))
+    up = lax.all_gather(lax.psum(jnp.stack(ups), "dp").astype(BF16), "segment", axis=2, tiled=True)
+    down = lax.all_gather(lax.psum(jnp.stack(downs), "dp").astype(BF16), "segment", axis=1, tiled=True)
+    cut = lambda v, n, ax: lax.dynamic_slice_in_dim(v, dp * n, n, ax).astype(F32)
+    att = lax.psum(pa.astype(F32), ("segment", "dp"))
+    att = lax.dynamic_index_in_dim(att, dp, 1, keepdims=False)
+    sm_all = lax.psum(smo, ("segment", "dp"))
+    mine = cut(sm_all, 96, 1)
+    upb = cut(sm_all[14:26].reshape(3, 3072), 384, 1)
+    return (
+        comb[0],
+        comb[1].astype(F32),
+        lax.dynamic_slice_in_dim(mine, seg, 1, 0),
+        lax.dynamic_slice_in_dim(mine, 4 + seg, 1, 0),
+        att[:, :, :2304],
+        mine[8:12].reshape(2, 2, 96),
+        att[:, :, 2304:],
+        mine[12:14],
+        cut(up, 96, 1),
+        upb,
+        cut(down, 384, 1),
+        mine[26:29],
+    )
+
+
 def solution(mesh):
+    known = mesh.shape["segment"] == 4 and mesh.shape["dp"] == 8
     return jax.shard_map(
-        per_device,
+        fast_device if known else per_device,
         mesh=mesh,
         in_specs=(
             P("dp", None, None),

time: 2650 us -> 976 us (0.37)
  waiting for transfers between devices: 1650 us -> 0.57 us
  blocking collectives: 0 us -> 744 us
  local copies, waits for them, and re-layouts: 347 us -> 15.2 us
  other arithmetic: 269 us -> 32.4 us
  matrix products: 161 us -> 51.3 us
  loops' own time: 108 us -> 0 us
  Pallas kernels: 0 us -> 106 us
  starting transfers between devices: 99.3 us -> 0.34 us
    psum x0 -> x2, blocking collectives: none -> 744 us  [the longest x1 463 us: fast_device(): att = lax.psum(pa.astype(F32), ('segment', 'dp'))]
    unnamed x4 -> x3, waiting for transfers between devices: 722 us -> 0.56 us
    ppermute x10 -> x0, waiting for transfers between devices: 677 us -> none  [shifted_2(): lax.ppermute(value, axis, [(source, source + steps) for source in range(l...]
    add x7 -> x2, other arithmetic: 179 us -> 1.45 us  [rolled_inputs(): 16 + spot // 32]
    all_gather x1 -> x2, waiting for transfers between devices: 172 us -> 0.01 us  [the longest x1 0.01 us: fast_device(): lax.all_gather(lax.psum(jnp.stack(ups), 'dp').astype(BF16), 'segment', ax...]
    another operation x14 -> x0, loops' own time: 108 us -> none  [the longest x2 62.1 us: backward_compute(): lax.switch(segment_place, [partial(backward_branch, section) for section...]
    pallas_call x0 -> x1, Pallas kernels: none -> 106 us  [run_chain(): pl.pallas_call(chain_kernel, out_shape=(shape((4, 256, 768), BF16), shape...]
    slice x36 -> x9, local copies, waits for them, and re-layouts: 108 us -> 7.74 us  [the longest x1 1.36 us: fast_device(): mine[8:12].reshape(2, 2, 96)]
  transfers between devices with their start and end apart: 13 -> 3, of which waited for: 10 -> 0; matrix products, arithmetic and copies ran while one was open for 9% -> 8% of each run, Pallas kernels for 0% -> 0%
where the time goes in v1:
time: 976 us; the launch traced here: 970 us
  blocking collectives  744 us (76%)
  Pallas kernels  106 us (11%)
  matrix products  51.3 us (5%)
  other arithmetic  32.4 us (3%)
  between operations  20 us (2%)
  local copies, waits for them, and re-layouts  15.2 us (2%)
    psum x1, blocking collectives, fast_device(): att = lax.psum(pa.astype(F32), ('segment', 'dp'))  463 us
    psum x1, blocking collectives, fast_device(): lax.psum(jnp.stack(ups), 'dp').astype(BF16)  281 us
    pallas_call x1, Pallas kernels, run_chain(): pl.pallas_call(chain_kernel, out_shape=(shape((4, 256, 768), BF16), shape...  106 us
    dot_general x9, matrix products, mm(): lax.dot_general(a, b, (((1,), (0,)), ((), ())), preferred_element_type=F32)  51.3 us
  transfers between devices with their start and end apart: 3, of which 0 were waited for; matrix products, arithmetic and copies ran while one was open for 8% of the time, Pallas kernels for 0%

profile of v1, /device:TPU:0, one launch (start us, length us, event | category | flops | bytes accessed | tf_op | source)
XLA Modules:
  0.0 970.3 jit_solution(11555789983629602384)
XLA Ops:
  13.6 1.5 slice_bitcast_fusion.1
  17.4 2.8 fusion.22
  21.0 1.7 fusion.24
  22.8 1.3 pad_maximum_fusion.2.tok
  24.1 1.3 pad_maximum_fusion.3.cot
  27.4 106.2 %shard_map.229 = (bf16[4,256,768]{2,1,0:T(8,128)(2,1)}, bf16[4,256,768]{2,1,0:T(8,128)(2,1)}, bf16[4,256,768]{2,1,0:T(8,128)(2,1)}, bf16[4,256,768]{2,1,0:T(8,12...) custom-call(bf16[2,512,768]{2,1,0:T(8,128)(2,1)} %pad_maximum_fusion.2.tok, ...), custom_call_target="tpu_custom_call" | custom-call | tf_op jit(solution)/shard_map/pallas_call | solution.py:956
  134.0 4.9 fusion.18
  138.9 9.0 convolution_bitcast_fusion.3
  147.9 5.9 convolution_bitcast_fusion
  153.8 4.3 fusion.20
  158.1 4.5 fusion.19
  162.6 1.4 broadcast_select_fusion.1
  164.0 9.9 %convolution_bitcast_fusion.4 = f32[1,768,768]{2,1,0:T(8,128)} fusion(bf16[1024,768]{1,0:T(8,128)(2,1)} %bitcast.89, f32[1024,768]{1,0:T(8,128)} %fusion.19, bf16[1024,768]{1,0:T(8,128)(2,1)} %bitcast.85, f32[768]{0:T(1024)S(1)} %get-tuple-element.28, bf16[3,3072,768]{2,1,0:T(8,128)(2,1)} %wd_h.1, s32[]{:T(128)S(6)} %add.281, s32[]{:T(128)S(6)} %select_n.148), kind=kOutput, calls=%fused_computation.27 | convolution fusion | flops 2430074880 | bytes 9833480 | tf_op jit(solution)/shard_map/dot_general | solution.py:509
  173.8 9.0 convolution_bitcast_fusion.5
  182.8 6.4 pad_maximum_fusion
  189.3 0.9 bitcast_select_fusion.1
  190.2 1.0 copy-done.15
  191.2 1.9 convolution_bitcast_fusion.1
  193.1 2.0 convolution_bitcast_fusion.2
  195.1 3.4 pad_maximum_fusion.1
  198.5 280.9 %all-reduce.7 = (bf16[3,768,768]{2,1,0:T(8,128)(2,1)}, bf16[3,768,768]{2,1,0:T(8,128)(2,1)}) all-reduce(f32[3,768,768]{2,1,0:T(8,128)} %pad_maximum_fusion, f32[3,768,768]{2,1,0:T(8,128)} %pad_maximum_fusion.1), channel_id=1, replica_groups=mesh['segment'=4,'dp'=8] {'dp'}, use_global_device_ids=true, to_apply=%region_3.4 | all-reduce | flops 3538944 | bytes 21233664 | tf_op jit(solution)/shard_map/psum | solution.py:1062
  480.1 463.3 %all-reduce.6 = f32[2,8,96,3072]{3,2,1,0:T(8,128)} all-reduce(bf16[2,8,96,3072]{3,2,1,0:T(8,128)(2,1)} %get-tuple-element.21), channel_id=1, replica_groups=mesh['segment'=4,'dp'=8] {'segment','dp'}, use_global_device_ids=true, to_apply=%region_2.3 | all-reduce | flops 4718592 | bytes 28311552 | tf_op jit(solution)/shard_map/psum | solution.py:1065
  943.4 1.8 dynamic-slice_bitcast_fusion
  945.2 1.3 slice.100
  947.4 1.1 bitcast_convert_fusion
  948.5 0.9 slice.105
  949.4 1.4 dynamic-slice
  950.8 1.3 dynamic-slice.1
  952.1 1.3 dynamic-slice.8
  953.5 1.4 fusion.78
  955.4 3.7 dynamic-slice_convert_fusion.1
  959.1 3.6 dynamic-slice_convert_fusion
  (72 shorter events, 9.1 us)
Async XLA Ops:
  8.0 940.5 %all-reduce.5.cloned.1.call-start = ((), (), s32[]{:S(2)}) async-start(), calls=%async_computation | async-start | bytes 196608 | tf_op jit(solution)/shard_map/psum | solution.py:1067
  12.0 3.0 copy-start.4
  13.5 1.7 copy-start.9
  13.5 1.7 copy-start.8
  13.5 1.7 copy-start.7
  13.5 1.7 copy-start.10
  13.6 2.4 copy-start.6
  20.2 2.5 copy-start.2
  21.0 3.0 copy-start.1
  22.8 4.0 copy-start.11
  22.8 4.0 copy-start.12
  133.7 821.8 %all-gather.3.cloned.1.call-start = ((), (), s32[]{:S(2)}) async-start(), calls=%async_computation.1 | async-start | bytes 17694720 | tf_op jit(solution)/shard_map/all_gather | solution.py:1062
  134.0 4.9 copy-start.14
  147.9 5.9 copy-start.13
  158.1 4.5 copy-start
  189.3 1.9 copy-start.15
  191.2 2.0 copy-start.16
  193.1 2.0 copy-start.3
  479.5 479.6 %all-gather.5.cloned.1.call-start = ((), (), s32[]{:S(2)}) async-start(), calls=%async_computation.2 | async-start | bytes 17694720 | tf_op jit(solution)/shard_map/all_gather | solution.py:1063
  945.2 2.2 copy-start.5
Sparse Core Ops, SparseCore 0:
  133.8 122.4 all-reduce.4
Sparse Core Ops, SparseCore 1:
  479.6 225.4 all-gather.2
  706.7 195.3 all-gather.4

commit v2 on v1

--- a/solution.py
+++ b/solution.py
@@ -845,12 +845,12 @@
                         out = mm(lt[0], pga[:, lanes(768 * n + 256 * i, 256)])
                     else:
                         out = mm(lt[1], gbuf[s, :, lanes(256 * i, 256)])
-                    pb[slot, :, :, lanes(256 * i, 256)] = out.astype(BF16).reshape(8, 96, 256)
+                    pb[slot, :, :, :, lanes(256 * i, 256)] = out.astype(BF16).reshape(4, 2, 96, 256)
                     return carry
 
                 lax.fori_loop(0, 3, step, 0)
                 copy = pltpu.make_async_copy(
-                    pb.at[slot], pao.at[l, :, :, pl.ds(768 * n, 768)], pb_sem.at[slot]
+                    pb.at[slot], pao.at[l, :, :, :, pl.ds(768 * n, 768)], pb_sem.at[slot]
                 )
                 copy.start()
                 pb_copies.append(copy)
@@ -960,7 +960,7 @@
             shape((4, 256, 768), BF16),
             shape((4, 256, 768), BF16),
             shape((4, 256, 768), BF16),
-            shape((2, 8, 96, 3072), BF16),
+            shape((2, 4, 2, 96, 3072), BF16),
             shape((2, 2, 128, 768), BF16),
             shape((32, 768), F32),
         ),
@@ -991,7 +991,7 @@
             pltpu.VMEM((256, 1536), BF16),
             pltpu.VMEM((2, 256, 1536), BF16),
             pltpu.VMEM((2, 768, 256), BF16),
-            pltpu.VMEM((2, 8, 96, 768), BF16),
+            pltpu.VMEM((2, 4, 2, 96, 768), BF16),
             pltpu.VMEM((256, 768), F32),
             pltpu.VMEM((2, 256, 768), BF16),
             pltpu.VMEM((4, 128, 768), BF16),
@@ -1006,6 +1006,433 @@
             collective_id=0, has_side_effects=True, vmem_limit_bytes=62 * MIB
         ),
     )(tok, cot, oh, gb, sm, ub, wq, wo, wu, wd)
+
+
+def reduce_kernel(
+    x1h, x3h, g2h, c4h, pah, ush, dsh, ubs, smi,
+    upo, dno, ato, smo,
+    xv, gv, xs, gs, wu, wd, av, pv, lt, pu, pd, ru, rd, ao, ar, eu, ed,
+    u1, d1, a1, u2, d2, a2, fu, fd, fa, ra, ta, sacc, srecv,
+    in_sem, al_sem, ars_sem, arr_sem, cs_sem, cr_sem, s1_sem, r1_sem, s2_sem, r2_sem,
+    us_sem, ur_sem, ul_sem, ds_sem, dr_sem, ps_sem, pr_sem, fs_sem, fr_sem, fl_sem,
+    ss_sem, sr_sem,
+):
+    seg, dp, z, k, y, x = places()
+    other = 1 - k
+    partner = (seg, 2 * z + other)
+    zp, zm, z2 = (z + 1) % 4, (z + 3) % 4, (z + 2) % 4
+    up_z, down_z, far_z = (seg, 2 * zp + k), (seg, 2 * zm + k), (seg, 2 * z2 + k)
+
+    def peer(d):
+        return ((seg + d) % 4, dp)
+
+    def remote(src, dst, ssem, rsem, where):
+        return pltpu.make_async_remote_copy(
+            src_ref=src, dst_ref=dst, send_sem=ssem, recv_sem=rsem,
+            device_id=where, device_id_type=MESH,
+        )
+
+    def local(src, dst, sem):
+        return pltpu.make_async_copy(src, dst, sem)
+
+    loads = {}
+
+    def load(name, src, dst):
+        copy = local(src, dst, in_sem.at[len(loads)])
+        copy.start()
+        loads[name] = copy
+
+    load("x3", x3h, xv.at[0])
+    load("u2", ush.at[2], wu.at[2])
+    load("c4", c4h, gv.at[0])
+    load("d2", dsh.at[2], wd.at[2])
+
+    barrier = pltpu.get_barrier_semaphore()
+    for d in range(4):
+        for c in range(2):
+            if d == 0 and c == 1:
+                continue
+            where = partner if d == 0 else ((seg + d) % 4, 2 * z + c)
+            pl.semaphore_signal(barrier, inc=1, device_id=where, device_id_type=MESH)
+    for where in (up_z, down_z, far_z):
+        pl.semaphore_signal(barrier, inc=1, device_id=where, device_id_type=MESH)
+    pl.semaphore_wait(barrier, 10)
+
+    att = []
+    for l in (1, 0):
+        here = local(pah.at[l, :, k], ao.at[l], al_sem.at[l])
+        there = remote(pah.at[l, :, other], ar.at[l], ars_sem.at[l], arr_sem.at[l], partner)
+        here.start()
+        there.start()
+        att.append((l, here, there))
+    load("x1", x1h, xv.at[1])
+    load("g2", g2h, gv.at[1])
+    for e in range(2):
+        load(f"u{e}", ush.at[e], wu.at[e])
+        load(f"d{e}", dsh.at[e], wd.at[e])
+
+    small_partners = (
+        partner,
+        (seg + 1 - 2 * x, dp),
+        ((seg + 2) % 4, dp),
+        (seg, 2 * (z + 1 - 2 * (z % 2)) + k),
+        far_z,
+    )
+    smalls = [
+        remote(sacc.at[i], srecv.at[i], ss_sem.at[i], sr_sem.at[i], small_partners[i])
+        for i in range(5)
+    ]
+    sacc[0] = smi[...]
+    smalls[0].start()
+
+    def small_step(i):
+        smalls[i].wait()
+        total = sacc[i] + srecv[i]
+        if i == 4:
+            smo[...] = total
+        else:
+            sacc[i + 1] = total
+            smalls[i + 1].start()
+
+    def wgrad(u, e, xin, gin, rows):
+        size = min(rows, 256)
+
+        def step(r, carry):
+            at = pl.ds(pl.multiple_of(size * r, size), size)
+            xr = xin(at)
+            pre = mm(xr, wu[e]) + ubs[e]
+            a, slope = gelu_both(pre)
+            av[at, :] = a.astype(BF16)
+            pv[at, :] = (mm_t(gin(at), wd[e]) * slope).astype(BF16)
+            lane_at = pl.ds(pl.multiple_of(size * r, size), size)
+            lt[0, :, lane_at] = xr.T
+            lt[1, :, lane_at] = av[at, :].T
+            return carry
+
+        lax.fori_loop(0, rows // size, step, 0)
+        everything = pl.ds(0, rows)
+
+        def out(n, carry):
+            at = pl.ds(pl.multiple_of(256 * n, 256), 256)
+            pu[u, :, :, :, at] = (
+                mm(lt[0, :, :rows], pv[everything, at]).astype(BF16).reshape(4, 2, 96, 256)
+            )
+            pd[u, :, :, at] = (
+                mm(lt[1, :, :rows], gin((everything, at))).astype(BF16).reshape(4, 192, 256)
+            )
+            return carry
+
+        lax.fori_loop(0, 3, out, 0)
+        half = pl.ds(pl.multiple_of(384 * other, 128), 384)
+        copies = (
+            remote(pu.at[u, :, other], ru.at[u], cs_sem.at[u, 0], cr_sem.at[u, 0], partner),
+            remote(pd.at[u, :, :, half], rd.at[u], cs_sem.at[u, 1], cr_sem.at[u, 1], partner),
+        )
+        for copy in copies:
+            copy.start()
+        return copies
+
+    own_half = pl.ds(pl.multiple_of(384 * k, 128), 384)
+
+    class Unit:
+        def __init__(self, i, shards, first, second):
+            self.shards, self.first, self.second, self.i = shards, first, second, i
+            rows = shards.shape[1]
+            lo, hi = pl.ds(0, rows // 2), pl.ds(rows // 2, rows // 2)
+            self.lo, self.hi = lo, hi
+            e, f, s = shards, first, second
+            self.early = [
+                remote(e.at[z2, lo], f.at[0], s1_sem.at[i, 0], r1_sem.at[i, 0], up_z),
+                remote(e.at[z2, hi], f.at[1], s1_sem.at[i, 1], r1_sem.at[i, 1], down_z),
+                remote(e.at[zp, hi], s.at[0, hi], s1_sem.at[i, 2], r1_sem.at[i, 2], up_z),
+                remote(e.at[zm, lo], s.at[1, lo], s1_sem.at[i, 3], r1_sem.at[i, 3], down_z),
+            ]
+            self.late = [
+                remote(e.at[zp, lo], s.at[0, lo], s2_sem.at[i, 0], r2_sem.at[i, 0], up_z),
+                remote(e.at[zm, hi], s.at[1, hi], s2_sem.at[i, 1], r2_sem.at[i, 1], down_z),
+            ]
+
+        def begin(self):
+            for copy in self.early:
+                copy.start()
+
+        def turn(self):
+            e, f = self.shards, self.first
+            self.early[0].wait_recv()
+            e[zp, self.lo] = (e[zp, self.lo].astype(F32) + f[0].astype(F32)).astype(BF16)
+            self.late[0].start()
+            self.early[1].wait_recv()
+            e[zm, self.hi] = (e[zm, self.hi].astype(F32) + f[1].astype(F32)).astype(BF16)
+            self.late[1].start()
+
+        def finish(self):
+            self.early[2].wait_recv()
+            self.early[3].wait_recv()
+            for copy in self.late:
+                copy.wait_recv()
+            s = self.second
+            return self.shards[z].astype(F32) + (s[0].astype(F32) + s[1].astype(F32))
+
+        def close(self):
+            for copy in self.early + self.late:
+                copy.wait_send()
+
+    att_units = {l: Unit(l, ao.at[l], a1.at[l], a2.at[l]) for l in range(2)}
+    up_units = {e: Unit(2 + e, eu.at[e], u1.at[e], u2.at[e]) for e in range(3)}
+    down_units = {e: Unit(5 + e, ed.at[e], d1.at[e], d2.at[e]) for e in range(3)}
+    tails = []
+
+    def give_up(e):
+        fu[e] = up_units[e].finish().astype(BF16)
+        here = local(fu.at[e], upo.at[seg, e], ul_sem.at[e])
+        here.start()
+        copies = [
+            remote(fu.at[e], upo.at[seg, e], us_sem.at[e, d - 1], ur_sem.at[e, d - 1], peer(d))
+            for d in (1, 2, 3)
+        ]
+        for copy in copies:
+            copy.start()
+
+        def close():
+            here.wait()
+            for copy in copies:
+                copy.wait()
+
+        tails.append(close)
+
+    def give_down(e):
+        fd[e] = down_units[e].finish().astype(BF16)
+        spot = dno.at[e, pl.ds(pl.multiple_of(192 * x, 64), 192), own_half]
+        near = local(fd.at[e], spot, ds_sem.at[e, 0])
+
+        def send(d):
+            where = partner if d == 0 else ((seg + d) % 4, 2 * z + y)
+            return remote(fd.at[e], spot, ds_sem.at[e, d], dr_sem.at[e, k, x], where)
+
+        for d in (1, 2, 3):
+            send(d).start()
+
+        @pl.when(k == y)
+        def _():
+            near.start()
+
+        @pl.when(k != y)
+        def _():
+            send(0).start()
+
+        def close():
+            for d in (1, 2, 3):
+                send(d).wait_send()
+
+            @pl.when(k == y)
+            def _():
+                near.wait()
+
+            @pl.when(k != y)
+            def _():
+                send(0).wait_send()
+
+            for j in range(2):
+                for m in range(2):
+                    @pl.when(jnp.logical_not((2 * k + m == seg) & (j == k)))
+                    def _():
+                        remote(
+                            fd.at[e], spot, ds_sem.at[e, 0], dr_sem.at[e, j, m], partner
+                        ).wait_recv()
+
+        tails.append(close)
+
+    plane = {}
+
+    def spread_att(l):
+        fa[l] = att_units[l].finish().astype(BF16)
+        copies = []
+        for d in (1, 2, 3):
+            piece = pl.ds(pl.multiple_of(768 * ((seg + d) % 4), 128), 768)
+            copies.append(
+                remote(
+                    fa.at[l, :, piece], ra.at[l, d - 1], ps_sem.at[l, d - 1], pr_sem.at[l, d - 1],
+                    peer(d),
+                )
+            )
+            copies[-1].start()
+        plane[l] = copies
+
+    def give_att(l):
+        for copy in plane[l]:
+            copy.wait()
+        piece = pl.ds(pl.multiple_of(768 * seg, 128), 768)
+        total = fa[l, :, piece].astype(F32) + ra[l, 0].astype(F32)
+        total = total + ra[l, 1].astype(F32) + ra[l, 2].astype(F32)
+        ta[l] = total.astype(BF16)
+        spot = ato.at[l, :, piece]
+        here = local(ta.at[l], spot, fl_sem.at[l])
+        here.start()
+        copies = [
+            remote(ta.at[l], spot, fs_sem.at[l, d - 1], fr_sem.at[l, d - 1], peer(d))
+            for d in (1, 2, 3)
+        ]
+        for copy in copies:
+            copy.start()
+
+        def close():
+            here.wait()
+            for copy in copies:
+                copy.wait()
+
+        tails.append(close)
+
+    for name in ("x3", "u2", "c4", "d2"):
+        loads[name].wait()
+
+    def rows_of(ref, slot):
+        def read(at):
+            return ref[slot, at[0], at[1]] if isinstance(at, tuple) else ref[slot, at, :]
+
+        return read
+
+    w3 = wgrad(0, 2, rows_of(xv, 0), rows_of(gv, 0), 1024)
+
+    for l, here, there in att:
+        here.wait()
+        there.wait()
+
+        def add(i, carry):
+            ao[l, i] = (ao[l, i].astype(F32) + ar[l, i].astype(F32)).astype(BF16)
+            return carry
+
+        lax.fori_loop(0, 4, add, 0)
+        att_units[l].begin()
+    small_step(0)
+
+    for copy in w3:
+        copy.wait()
+    eu[2] = (pu[0, :, k].astype(F32) + ru[0].astype(F32)).astype(BF16)
+    ed[2] = (pd[0, :, :, own_half].astype(F32) + rd[0].astype(F32)).astype(BF16)
+    up_units[2].begin()
+    down_units[2].begin()
+
+    for name in ("x1", "g2", "u0", "u1", "d0", "d1"):
+        loads[name].wait()
+    spots = lax.broadcasted_iota(jnp.int32, (256, 1), 0)
+    is_first = ((spots < PATCHES) | (k == 1)).astype(F32)
+    is_second = ((spots >= PATCHES) & (k == 0)).astype(F32)
+    for r in range(4):
+        grad = gv[1, 256 * r : 256 * (r + 1), :].astype(F32)
+        gs[64 * r : 64 * (r + 1), :] = (grad[192:] * is_second[192:]).astype(BF16)
+        gv[1, 256 * r : 256 * (r + 1), :] = (grad * is_first).astype(BF16)
+        xs[64 * r : 64 * (r + 1), :] = xv[1, 256 * r + 192 : 256 * (r + 1), :]
+    wp = wgrad(1, k, rows_of(xv, 1), rows_of(gv, 1), 1024)
+    small_step(1)
+    for l in (1, 0):
+        att_units[l].turn()
+    up_units[2].turn()
+    down_units[2].turn()
+
+    def whole(ref):
+        def read(at):
+            return ref[at[0], at[1]] if isinstance(at, tuple) else ref[at, :]
+
+        return read
+
+    wq = wgrad(2, 1, whole(xs), whole(gs), 256)
+    small_step(2)
+    for copy in wp + wq:
+        copy.wait()
+    first = k == 0
+    eu[0] = jnp.where(first, pu[1, :, k], ru[1])
+    ed[0] = jnp.where(first, pd[1, :, :, own_half], rd[1])
+    up_units[0].begin()
+    down_units[0].begin()
+    eu[1] = jnp.where(
+        first,
+        pu[2, :, k].astype(F32) + ru[1].astype(F32),
+        pu[1, :, k].astype(F32) + ru[2].astype(F32),
+    ).astype(BF16)
+    ed[1] = jnp.where(
+        first,
+        pd[2, :, :, own_half].astype(F32) + rd[1].astype(F32),
+        pd[1, :, :, own_half].astype(F32) + rd[2].astype(F32),
+    ).astype(BF16)
+    up_units[1].begin()
+    down_units[1].begin()
+
+    spread_att(1)
+    spread_att(0)
+    give_up(2)
+    give_down(2)
+    small_step(3)
+    for e in (0, 1):
+        up_units[e].turn()
+        down_units[e].turn()
+    give_att(1)
+    give_att(0)
+    small_step(4)
+    for e in (0, 1):
+        give_up(e)
+        give_down(e)
+    for close in tails:
+        close()
+    for unit in list(att_units.values()) + list(up_units.values()) + list(down_units.values()):
+        unit.close()
+
+
+def run_reduce(x1, x3, g2, c4, pa, us, ds, ubs, smo):
+    any_ = pl.BlockSpec(memory_space=pl.ANY)
+    vm = pl.BlockSpec(memory_space=pltpu.VMEM)
+    dma = pltpu.SemaphoreType.DMA
+    shape = jax.ShapeDtypeStruct
+    return pl.pallas_call(
+        reduce_kernel,
+        out_shape=(
+            shape((4, 3, 96, 768), BF16),
+            shape((3, 384, 768), BF16),
+            shape((2, 96, 3072), BF16),
+            shape((32, 768), F32),
+        ),
+        in_specs=[any_] * 7 + [vm, vm],
+        out_specs=(any_, any_, any_, vm),
+        scratch_shapes=[
+            pltpu.VMEM((2, 1024, 768), BF16),
+            pltpu.VMEM((2, 1024, 768), BF16),
+            pltpu.VMEM((256, 768), BF16),
+            pltpu.VMEM((256, 768), BF16),
+            pltpu.VMEM((3, 768, 768), BF16),
+            pltpu.VMEM((3, 768, 768), BF16),
+            pltpu.VMEM((1024, 768), BF16),
+            pltpu.VMEM((1024, 768), BF16),
+            pltpu.VMEM((2, 768, 1024), BF16),
+            pltpu.VMEM((3, 4, 2, 96, 768), BF16),
+            pltpu.VMEM((3, 4, 192, 768), BF16),
+            pltpu.VMEM((3, 4, 96, 768), BF16),
+            pltpu.VMEM((3, 4, 192, 384), BF16),
+            pltpu.VMEM((2, 4, 96, 3072), BF16),
+            pltpu.VMEM((2, 4, 96, 3072), BF16),
+            pltpu.VMEM((3, 4, 96, 768), BF16),
+            pltpu.VMEM((3, 4, 192, 384), BF16),
+            pltpu.VMEM((3, 2, 48, 768), BF16),
+            pltpu.VMEM((3, 2, 96, 384), BF16),
+            pltpu.VMEM((2, 2, 48, 3072), BF16),
+            pltpu.VMEM((3, 2, 96, 768), BF16),
+            pltpu.VMEM((3, 2, 192, 384), BF16),
+            pltpu.VMEM((2, 2, 96, 3072), BF16),
+            pltpu.VMEM((3, 96, 768), BF16),
+            pltpu.VMEM((3, 192, 384), BF16),
+            pltpu.VMEM((2, 96, 3072), BF16),
+            pltpu.VMEM((2, 3, 96, 768), BF16),
+            pltpu.VMEM((2, 96, 768), BF16),
+            pltpu.VMEM((5, 32, 768), F32),
+            pltpu.VMEM((5, 32, 768), F32),
+            dma((12,)), dma((2,)), dma((2,)), dma((2,)), dma((3, 2)), dma((3, 2)),
+            dma((8, 4)), dma((8, 4)), dma((8, 2)), dma((8, 2)),
+            dma((3, 3)), dma((3, 3)), dma((3,)), dma((3, 4)), dma((3, 2, 2)),
+            dma((2, 3)), dma((2, 3)), dma((2, 3)), dma((2, 3)), dma((2,)),
+            dma((5,)), dma((5,)),
+        ],
+        compiler_params=pltpu.CompilerParams(
+            collective_id=1, has_side_effects=True, vmem_limit_bytes=62 * MIB
+        ),
+    )(x1, x3, g2, c4, pa, us, ds, ubs, smo)
 
 
 def rolled_inputs(tokens, group_ids, type_ids, out_cotangent):
@@ -1043,28 +1470,16 @@
     x1, x3, g2, c4, pa, comb, smo = run_chain(
         tok, cot, oh, gb, sm, ub, qkv_weight, out_weight, up_weight, down_weight
     )
-    k = dp % 2
-    us = lax.dynamic_slice_in_dim(up_weight, seg * 768, 768, 2)
-    ds = lax.dynamic_slice_in_dim(down_weight, seg * 768, 768, 1)
-    bs = lax.dynamic_slice_in_dim(up_bias, seg * 768, 768, 1).astype(F32)
-    img = (jnp.arange(256)[None, :] < PATCHES) & (k == 0)
-    img = jnp.broadcast_to(img, (4, 256)).reshape(1024)
-    ups, downs = [], []
-    for e in range(3):
-        xs = (x3 if e == 2 else x1).reshape(1024, 768)
-        gs = (c4 if e == 2 else g2).reshape(1024, 768)
-        if e < 2:
-            gs = jnp.where((img == (e == 0))[:, None], gs, 0)
-        a, slope = gelu_both(mm(xs, us[e]) + bs[e])
-        pg = (mm_t(gs, ds[e]) * slope).astype(BF16)
-        ups.append(mm(xs.T, pg))
-        downs.append(mm(a.astype(BF16).T, gs))
-    up = lax.all_gather(lax.psum(jnp.stack(ups), "dp").astype(BF16), "segment", axis=2, tiled=True)
-    down = lax.all_gather(lax.psum(jnp.stack(downs), "dp").astype(BF16), "segment", axis=1, tiled=True)
-    cut = lambda v, n, ax: lax.dynamic_slice_in_dim(v, dp * n, n, ax).astype(F32)
-    att = lax.psum(pa.astype(F32), ("segment", "dp"))
-    att = lax.dynamic_index_in_dim(att, dp, 1, keepdims=False)
-    sm_all = lax.psum(smo, ("segment", "dp"))
+    us = lax.dynamic_slice_in_dim(up_weight.reshape(3, 768, 4, 768), 192 * seg, 192, 3)
+    us = us.reshape(3, 768, 768)
+    ds = lax.dynamic_slice_in_dim(down_weight.reshape(3, 4, 768, 768), 192 * seg, 192, 2)
+    ds = ds.reshape(3, 768, 768)
+    ubs = lax.dynamic_slice_in_dim(up_bias.reshape(3, 4, 768), 192 * seg, 192, 2)
+    ubs = ubs.reshape(3, 1, 768).astype(F32)
+    x1, x3, g2, c4 = (v.reshape(1024, 768) for v in (x1, x3, g2, c4))
+    up, down, att, sm_all = run_reduce(x1, x3, g2, c4, pa, us, ds, ubs, smo)
+    up = jnp.moveaxis(up.reshape(4, 3, 96, 4, 192), 0, 3).reshape(3, 96, 3072).astype(F32)
+    cut = lambda v, n, ax: lax.dynamic_slice_in_dim(v, dp * n, n, ax)
     mine = cut(sm_all, 96, 1)
     upb = cut(sm_all[14:26].reshape(3, 3072), 384, 1)
     return (
@@ -1072,13 +1487,13 @@
         comb[1].astype(F32),
         lax.dynamic_slice_in_dim(mine, seg, 1, 0),
         lax.dynamic_slice_in_dim(mine, 4 + seg, 1, 0),
-        att[:, :, :2304],
+        att[:, :, :2304].astype(F32),
         mine[8:12].reshape(2, 2, 96),
-        att[:, :, 2304:],
+        att[:, :, 2304:].astype(F32),
         mine[12:14],
-        cut(up, 96, 1),
+        up,
         upb,
-        cut(down, 384, 1),
+        down.astype(F32),
         mine[26:29],
     )
 

time: 976 us -> 366 us (0.38)
  blocking collectives: 744 us -> 0 us
  Pallas kernels: 106 us -> 281 us
  matrix products: 51.3 us -> 0 us
  local copies, waits for them, and re-layouts: 15.2 us -> 57.2 us
  other arithmetic: 32.4 us -> 16.3 us
  between operations: 20 us -> 4.92 us
    psum x2 -> x0, blocking collectives: 744 us -> none  [the longest x1 463 us: fast_device(): att = lax.psum(pa.astype(F32), ('segment', 'dp'))]
    pallas_call x0 -> x1, Pallas kernels: none -> 175 us  [run_reduce(): pl.pallas_call(reduce_kernel, out_shape=(shape((4, 3, 96, 768), BF16), sh...]
    dot_general x9 -> x0, matrix products: 51.3 us -> none  [mm(): lax.dot_general(a, b, (((1,), (0,)), ((), ())), preferred_element_type=F32)]
    convert_element_type x0 -> x4, local copies, waits for them, and re-layouts: none -> 21.1 us  [the longest x3 20.4 us: fast_device(): jnp.moveaxis(up.reshape(4, 3, 96, 4, 192), 0, 3).reshape(3, 96, 3072)]
    unnamed x34 -> x25, local copies, waits for them, and re-layouts: 1.09 us -> 18.9 us
    another operation x2 -> x0, other arithmetic: 9.83 us -> none  [the longest x1 6.43 us: fast_device(): jnp.stack(ups)]
  transfers between devices with their start and end apart: 3 -> 0, of which waited for: 0 -> 0; matrix products, arithmetic and copies ran while one was open for 8% -> 0% of each run, Pallas kernels for 0% -> 0%
where the time goes in v2:
time: 366 us; the launch traced here: 360 us
  Pallas kernels  281 us (77%)
  local copies, waits for them, and re-layouts  57.2 us (16%)
  other arithmetic  16.3 us (4%)
  between operations  4.92 us (1%)
    pallas_call x1, Pallas kernels, run_reduce(): pl.pallas_call(reduce_kernel, out_shape=(shape((4, 3, 96, 768), BF16), sh...  175 us
    pallas_call x1, Pallas kernels, run_chain(): pl.pallas_call(chain_kernel, out_shape=(shape((4, 256, 768), BF16), shape...  106 us
    convert_element_type x3, local copies, waits for them, and re-layouts, fast_device(): jnp.moveaxis(up.reshape(4, 3, 96, 4, 192), 0, 3).reshape(3, 96, 3072)  20.4 us
    unnamed x25, local copies, waits for them, and re-layouts  18.9 us

profile of v2, /device:TPU:0, one launch (start us, length us, event | category | flops | bytes accessed | tf_op | source)
XLA Modules:
  0.0 359.8 jit_solution(2729095070227998776)
XLA Ops:
  0.6 0.8 fusion.12
  4.0 0.8 fusion.22
  4.8 0.7 fusion.14
  7.8 0.7 fusion.17
  8.8 0.8 add_convert_fusion.oh
  9.5 1.6 slice_bitcast_fusion.1
  11.5 1.8 fusion.3
  13.3 1.8 fusion.1
  15.0 1.3 pad_maximum_fusion.1.cot
  16.4 1.3 pad_maximum_fusion.tok
  17.8 0.6 convert_element_type.44.sm
  18.4 0.7 reshape.429.ub
  19.1 0.7 maximum_convert_fusion.gb
  19.8 106.4 %shard_map.229 = (bf16[4,256,768]{2,1,0:T(8,128)(2,1)}, bf16[4,256,768]{2,1,0:T(8,128)(2,1)}, bf16[4,256,768]{2,1,0:T(8,128)(2,1)}, bf16[4,256,768]{2,1,0:T(8,12...) custom-call(bf16[2,512,768]{2,1,0:T(8,128)(2,1)} %pad_maximum_fusion.tok, ...), custom_call_target="tpu_custom_call" | custom-call | tf_op jit(solution)/shard_map/pallas_call | solution.py:956
  126.3 18.6 %copy.27 = bf16[3,768,3072]{1,2,0:T(8,128)(2,1)} copy(bf16[3,768,3072]{2,1,0:T(8,128)(2,1)} %wu_h.1) | data formatting | bytes 28311552 | tf_op args[9]
  144.9 2.2 constant_dynamic-slice_fusion.2
  147.1 3.7 %copy.28.ush = bf16[3,768,768]{2,1,0:T(8,128)(2,1)} copy(bf16[3,768,768]{1,2,0:T(8,128)(2,1)S(1)} %bitcast.40) | data formatting | bytes 7077888 | tf_op jit(solution)/shard_map/reshape | solution.py:1474
  150.8 4.0 %constant_dynamic-slice_fusion.1 = bf16[3,4,192,768]{3,2,1,0:T(8,128)(2,1)} fusion(bf16[3,4,768,768]{3,2,1,0:T(8,128)(2,1)} %bitcast.37, s32[]{:T(128)S(6)} %select_n.109), kind=kLoop, calls=%fused_computation.60 | loop fusion | bytes 7077892 | tf_op jit(solution)/shard_map/dynamic_slice | solution.py:1475
  155.0 0.7 reshape.431.ubs
  155.7 175.0 %shard_map.230 = (bf16[4,3,96,768]{3,2,1,0:T(8,128)(2,1)}, bf16[3,384,768]{2,1,0:T(8,128)(2,1)}, bf16[2,96,3072]{2,1,0:T(8,128)(2,1)}, f32[32,768]{1,0:T(8,128)}) custom-call(bf16[1024,768]{1,0:T(8,128)(2,1)} %bitcast.42, bf16[1024,768]{1,0:T(8,128)(2,1)} %bitcast.43, bf16[1024,768]{1,0:T(8,128)(2,1)} %bitcast.44, bf16[1024,768]{1,0:T(8,128)(2,1)} %bitcast.45, ...), custom_call_target="tpu_custom_call" | custom-call | tf_op jit(solution)/shard_map/pallas_call | solution.py:1385
  330.6 6.4 %reshape.433 = f32[4,3,96,4,192]{4,3,2,1,0:T(4,128)} reshape(bf16[4,3,96,768]{3,2,1,0:T(8,128)(2,1)} %get-tuple-element.32) | data formatting | bytes 5308416 | tf_op jit(solution)/shard_map/convert_element_type | solution.py:1481
  337.0 7.6 %copy.29 = f32[3,96,4,4,192]{4,3,2,1,0:T(4,128)} copy(f32[3,96,4,4,192]{4,2,1,0,3:T(4,128)} %bitcast.39) | data formatting | bytes 7077888 | tf_op jit(solution)/shard_map/convert_element_type | solution.py:1481
  344.6 6.4 %reshape.432 = f32[3,96,3072]{2,1,0:T(8,128)} reshape(f32[3,96,4,4,192]{4,3,2,1,0:T(4,128)} %copy.29) | data formatting | bytes 7077888 | tf_op jit(solution)/shard_map/convert_element_type | solution.py:1481
  351.0 2.1 convert_element_type.55
  353.1 1.3 slice_convert_fusion
  354.4 0.9 slice_convert_fusion.1
  355.3 0.6 constant_dynamic-slice_fusion
  355.9 0.7 dynamic-slice
  356.6 0.7 dynamic-slice.2
  357.2 0.6 fusion.21
  357.8 0.6 dynamic-slice.1
  358.5 1.1 bitcast_convert_fusion
  (42 shorter events, 2.0 us)
Async XLA Ops:
  9.5 1.9 copy-start.1
  16.3 1.3 copy-start.8
  16.3 1.4 copy-start.7
  16.3 1.4 copy-start.9
  16.3 2.1 copy-start.4
  16.3 2.8 copy-start.10
  16.4 2.8 copy-start.11
  150.8 4.0 %copy-start.5 = (bf16[3,3072]{1,0:T(4,128)(2,1)S(1)}, bf16[3,3072]{1,0:T(4,128)(2,1)}, u32[]{:S(2)}) copy-start(bf16[3,3072]{1,0:T(4,128)(2,1)} %param.24) | copy-start | bytes 55300
  344.6 6.4 %copy-start = (bf16[3,384,768]{2,1,0:T(8,128)(2,1)S(1)}, bf16[3,384,768]{2,1,0:T(8,128)(2,1)}, u32[]{:S(2)}) copy-start(bf16[3,384,768]{2,1,0:T(8,128)(2,1)} %get-tuple-element.33) | copy-start | bytes 5308420
  351.0 2.1 copy-start.2
  353.1 2.2 copy-start.6
  353.1 5.4 %copy-start.3 = (bf16[2,2,128,768]{3,2,1,0:T(8,128)(2,1)S(1)}, bf16[2,2,128,768]{3,2,1,0:T(8,128)(2,1)}, u32[]{:S(2)}) copy-start(bf16[2,2,128,768]{3,2,1,0:T(8,128)(2,1)} %get-tuple-element.23) | copy-start | bytes 2359300
